TPU v7x, 128 devices: a whole 4x4x4 slice. The times are simulated.
128 devices in a mesh: ep: 16 (over y, x), wide: 8 (over z, core).
Axes of the slice: x: 4, y: 4, z: 4, core: 2. Of those that a mesh axis runs over, the one named last changes fastest.
Arguments:
- requests: bfloat16 [2, 1024, 7168], P(None, ('ep', 'wide')), may hold values from -6 to 6
- routes: int32 [2, 1024, 2], P(None, ('ep', 'wide')), may hold values from 0 to 15, all different within a row
- gates: bfloat16 [2, 1024, 2], P(None, ('ep', 'wide')), may hold values from 0.099609375 to 1
- replica: int32 [1024, 2], P(('ep', 'wide')), may hold values from 0 to 3
- placement: int32 [16], replicated, may hold values from 0 to 15, each once
- copy_plan: int32 [4], replicated, may hold values from 0 to 15, as said below
- capacity: int32 [2, 16], replicated, may hold values from 8 to 16, as said below
- gate_proj: bfloat16 [16, 7168, 2048], P('ep', None, 'wide'), may hold values from -0.0625 to 0.0625
- up_proj: bfloat16 [16, 7168, 2048], P('ep', None, 'wide'), may hold values from -0.0625 to 0.0625
- down_proj: bfloat16 [16, 2048, 7168], P('ep', 'wide'), may hold values from -0.125 to 0.125
Outputs:
- moe_out: bfloat16 [2, 1024, 7168], P(None, ('ep', 'wide'))
Inputs may be any that keep to these rules, and one draw needn't show every extreme that they name: `copy_plan`: entries 1 to 3 are the distances 1, half of 16 and 15, in some order. `capacity`: no more than 16, which some device reaches in each step. `routes`: each row names 2 different experts.
All inputs are finite; a program needn't handle non-finite values.
Results may differ from a plain program's by a relative error of at most 0.02.
Values may be sent and summed in bfloat16 or wider, within the bound.
A program may use at most 128 MiB of HBM per device.

v0:
```python
import jax
import jax.numpy as jnp
from jax import lax
from jax.sharding import PartitionSpec as P

STEPS = 2
CAP = 16


def broadcast(x, axis, root):
    mine = lax.axis_index(axis) == root
    return lax.psum(jnp.where(mine, x, jnp.zeros_like(x)), axis)


def plan_group(
    ids, chooser, placement, hot_expert, new_owners, limits, second, experts, slot_count
):
    slots = jnp.arange(experts, dtype=jnp.int32)
    server = jnp.sum(jnp.where(ids[..., None] == slots, placement, 0), -1, dtype=jnp.int32)
    copied = jnp.zeros(ids.shape, jnp.int32)
    if second:
        hot = hot_expert[0]
        hot_home = jnp.sum(jnp.where(slots == hot, placement, 0), dtype=jnp.int32)
        candidates = jnp.concatenate([hot_home[None], new_owners])
        listed = jnp.arange(candidates.shape[0], dtype=jnp.int32)
        chosen = jnp.sum(
            jnp.where(chooser[..., None] == listed, candidates, 0), -1, dtype=jnp.int32
        )
        is_hot = ids == hot
        server = jnp.where(is_hot, chosen, server)
        copied = (is_hot & (chooser > 0)).astype(jnp.int32)
    server = server.reshape(-1)
    copied = copied.reshape(-1)
    onehot = (server[:, None] == slots).astype(jnp.int32)
    before = jnp.cumsum(onehot, 0, dtype=jnp.int32) - onehot
    position = jnp.sum(before * onehot, -1, dtype=jnp.int32)
    limit = jnp.sum(onehot * limits, -1, dtype=jnp.int32)
    kept = (position < limit).astype(jnp.int32)
    places = jnp.arange(slot_count, dtype=jnp.int32)
    match = (
        kept[:, None, None]
        * onehot[:, :, None]
        * (position[:, None, None] == places).astype(jnp.int32)
    )
    return (match, copied)


def run_expert(rows, gate_w, up_w, down_w):
    gate = jnp.dot(rows, gate_w, preferred_element_type=jnp.float32)
    upper = jnp.dot(rows, up_w, preferred_element_type=jnp.float32)
    hidden = (jax.nn.silu(gate) * upper).astype(jnp.bfloat16)
    return jnp.dot(hidden, down_w, preferred_element_type=jnp.float32)


def shards(
    requests, routes, gates, replica, placement, copy_plan, capacity, gate_proj, up_proj, down_proj
):
    n_ep = lax.axis_size("ep")
    n_wide = lax.axis_size("wide")
    width = requests.shape[2]
    home_w = (gate_proj[0], up_proj[0], down_proj[0])
    slots = jnp.arange(n_ep, dtype=jnp.int32)
    hot_expert = copy_plan[:1]
    hot_slot = jnp.sum(jnp.where(slots == hot_expert[0], placement, 0), dtype=jnp.int32)
    new_owners = (hot_slot + copy_plan[1:]) % n_ep
    is_owner = jnp.any(new_owners == lax.axis_index("ep"))
    copies = (
        broadcast(home_w[0], "ep", hot_slot),
        broadcast(home_w[1], "ep", hot_slot),
        broadcast(home_w[2], "ep", hot_slot),
    )
    block = CAP // n_wide
    wide_pos = lax.axis_index("wide")
    results = []
    for step_index in range(STEPS):
        second = step_index == 1
        rows_all, ids_all, chooser_all, gate_all = (
            lax.all_gather(requests[step_index], "wide", axis=0, tiled=True),
            lax.all_gather(routes[step_index], "wide", axis=0, tiled=True),
            lax.all_gather(replica, "wide", axis=0, tiled=True),
            lax.all_gather(gates[step_index], "wide", axis=0, tiled=True),
        )
        group = rows_all.shape[0]
        picks = ids_all.shape[1]
        match, copied = plan_group(
            ids_all,
            chooser_all,
            placement,
            hot_expert,
            new_owners,
            capacity[step_index],
            second,
            n_ep,
            CAP,
        )
        match_float = match.astype(jnp.float32)
        dispatch = match_float.reshape(group, picks, n_ep * CAP).sum(1)
        outgoing = lax.dot_general(
            dispatch.astype(jnp.bfloat16),
            rows_all,
            (((0,), (0,)), ((), ())),
            preferred_element_type=jnp.float32,
        )
        outgoing = outgoing.astype(jnp.bfloat16).reshape(n_ep, CAP, width)
        tags = jnp.sum(match * copied[:, None, None], 0, dtype=jnp.int32)
        weighting = match_float * gate_all.astype(jnp.float32).reshape(-1)[:, None, None]
        weighting = weighting.reshape(group, picks, n_ep, CAP).sum(1)
        rows_in = lax.all_to_all(outgoing, "ep", split_axis=0, concat_axis=0, tiled=True)
        tags_in = lax.all_to_all(tags, "ep", split_axis=0, concat_axis=0, tiled=True)
        count = rows_in.shape[1]
        flat = rows_in.reshape(-1, width)
        result = run_expert(flat, home_w[0], home_w[1], home_w[2])
        if second:

            def with_copy(values):
                other = run_expert(values[0], copies[0], copies[1], copies[2])
                return jnp.where(tags_in.reshape(-1, 1) > 0, other, values[1])

            result = lax.cond(is_owner, with_copy, lambda values: values[1], (flat, result))
        partial_out = result.reshape(n_ep, count, width)
        returned = lax.all_to_all(
            partial_out.astype(jnp.bfloat16), "ep", split_axis=0, concat_axis=0, tiled=True
        )
        slot_out = lax.psum_scatter(
            returned.astype(jnp.float32).astype(jnp.bfloat16),
            "wide",
            scatter_dimension=1,
            tiled=True,
        )
        share = lax.dynamic_slice_in_dim(weighting, wide_pos * block, block, 2)
        row_terms = jnp.dot(
            share.reshape(group, -1),
            slot_out.reshape(-1, width).astype(jnp.float32),
            precision=lax.Precision.HIGHEST,
        )
        mine = lax.psum_scatter(
            row_terms.astype(jnp.bfloat16), "wide", scatter_dimension=0, tiled=True
        )
        results.append(mine)
    return jnp.stack(results)


def solution(mesh):
    placed = (
        P(None, ("ep", "wide"), None),
        P(None, ("ep", "wide"), None),
        P(None, ("ep", "wide"), None),
        P(("ep", "wide"), None),
        P(),
        P(),
        P(),
        P("ep", None, "wide"),
        P("ep", None, "wide"),
        P("ep", "wide", None),
    )
    return jax.shard_map(
        shards, mesh=mesh, in_specs=placed, out_specs=P(None, ("ep", "wide"), None), check_vma=False
    )
```

profile of v0, /device:TPU:1, one launch (start us, length us, event | category | flops | bytes accessed | tf_op | source)
XLA Modules:
  0.0 493.1 jit_solution(18008591136985895774)
XLA Ops:
  7.4 1.9 fusion.59
  10.0 4.3 bitcast_select_fusion
  14.3 1.3 copy-done.3
  15.6 3.4 bitcast_select_fusion.1
  19.0 0.6 copy-done.6
  19.6 1.4 compare_reduce_fusion
  21.1 13.1 %all-gather.6 = s32[8,8,2]{1,2,0:T(2,128)S(1)} all-gather(s32[1,8,2]{1,2,0:T(2,128)S(1)} %bitcast.105), channel_id=1, replica_groups=mesh['ep'=16,'wide'=8] {'wide'}, dimensions={0}, use_global_device_ids=true | all-gather | bytes 576 | tf_op jit(solution)/shard_map/all_gather | solution.py:80
  34.4 12.8 %all-gather.3 = s32[1,64,2]{2,0,1:T(1,128)S(1)} all-gather(s32[1,8,2]{2,0,1:T(1,128)S(1)} %copy.124), channel_id=5, replica_groups=mesh['ep'=16,'wide'=8] {'wide'}, dimensions={1}, use_global_device_ids=true | all-gather | bytes 576 | tf_op jit(solution)/shard_map/all_gather | solution.py:79
  47.3 12.8 %all-gather = s32[1,64,2]{2,0,1:T(1,128)S(1)} all-gather(s32[1,8,2]{2,0,1:T(1,128)S(1)} %copy.121), channel_id=2, replica_groups=mesh['ep'=16,'wide'=8] {'wide'}, dimensions={1}, use_global_device_ids=true | all-gather | bytes 576 | tf_op jit(solution)/shard_map/all_gather | solution.py:79
  60.2 0.7 pad_add_fusion
  61.2 0.1 copy.112
  61.2 0.1 eq.197
  61.5 0.1 copy.100
  61.6 0.1 eq.174
  61.8 0.2 reduce_window_sum.18
  62.0 0.2 reduce_window_sum.17
  62.2 0.2 select_reduce_fusion
  62.6 0.3 multiply_convert_fusion.1
  62.9 0.5 convert_element_type.130
  63.5 0.2 reduce_sum.135
  63.7 13.6 %all-gather.2 = bf16[1,64,7168]{2,1,0:T(8,128)(2,1)S(1)} all-gather(bf16[1,8,7168]{2,1,0:T(8,128)(2,1)S(1)} %get-tuple-element.63), channel_id=4, replica_groups=mesh['ep'=16,'wide'=8] {'wide'}, dimensions={1}, use_global_device_ids=true | all-gather | bytes 1032192 | tf_op jit(solution)/shard_map/all_gather | solution.py:78
  77.3 1.1 convolution_convert_fusion.2
  78.4 62.7 %all_to_all.29 = bf16[16,16,7168]{2,1,0:T(8,128)(2,1)S(1)} all-to-all(bf16[16,16,7168]{2,1,0:T(8,128)(2,1)S(1)} %bitcast.93), channel_id=1, replica_groups=mesh['ep'=16,'wide'=8] {'ep'}, dimensions={0} | all-to-all | bytes 7340032 | tf_op jit(solution)/shard_map/all_to_all | solution.py:108
  141.2 1.1 fusion.19
  142.3 0.9 copy-done.2
  143.2 1.2 fusion.32
  144.4 0.9 copy-done
  145.2 1.1 convolution_convert_fusion.1
  146.4 3.9 copy.107
  150.3 4.7 all-to-all-start.1
  155.1 0.1 copy.118
  155.2 0.1 reshape.236
  155.5 1.1 fusion.35
  156.6 0.5 convert_element_type.145
  157.1 0.2 reduce_sum.144
  157.3 15.0 %all-gather.5 = bf16[1,64,7168]{2,1,0:T(8,128)(2,1)S(1)} all-gather(bf16[1,8,7168]{2,1,0:T(8,128)(2,1)S(1)} %get-tuple-element.64), channel_id=7, replica_groups=mesh['ep'=16,'wide'=8] {'wide'}, dimensions={1}, use_global_device_ids=true | all-gather | bytes 1032192 | tf_op jit(solution)/shard_map/all_gather | solution.py:78
  172.3 2.9 convolution_convert_fusion
  175.2 40.9 %all-to-all-done.1 = bf16[16,16,7168]{2,1,0:T(8,128)(2,1)} async-done(((bf16[16,16,7168]{2,1,0:T(8,128)(2,1)}), bf16[16,16,7168]{2,1,0:T(8,128)(2,1)}, u32[]{:S(2)}, u32[]{:S(2)}) %all-to-all-start.1) | async-done | bytes 3670048 | tf_op jit(solution)/shard_map/all_to_all | solution.py:121
  216.0 5.1 %all-to-all-start.2 = ((bf16[16,16,7168]{2,1,0:T(8,128)(2,1)}), bf16[16,16,7168]{2,1,0:T(8,128)(2,1)}, u32[]{:S(2)}, u32[]{:S(2)}) async-start(bf16[16,16,7168]{2,1,0:T(8,128)(2,1)} %bitcast.92), calls=%async_computation.4 | async-start | bytes 7340032 | tf_op jit(solution)/shard_map/all_to_all | solution.py:108
  221.2 6.1 %copy.108 = bf16[16,16,7168]{2,0,1:T(8,128)(2,1)} copy(bf16[16,16,7168]{2,1,0:T(8,128)(2,1)} %all-to-all-done.1) | data formatting | bytes 7340032 | tf_op jit(solution)/shard_map/all_to_all | solution.py:121
  227.9 68.1 %all-to-all-done.2 = bf16[16,16,7168]{2,1,0:T(8,128)(2,1)} async-done(((bf16[16,16,7168]{2,1,0:T(8,128)(2,1)}), bf16[16,16,7168]{2,1,0:T(8,128)(2,1)}, u32[]{:S(2)}, u32[]{:S(2)}) %all-to-all-start.2) | async-done | bytes 3670048 | tf_op jit(solution)/shard_map/all_to_all | solution.py:108
  296.0 4.0 all-to-all-start.3
  300.0 4.3 fusion.17
  304.3 10.0 %fusion.11 = bf16[256,7168]{1,0:T(8,128)(2,1)} fusion(bf16[1,256,7168]{2,1,0:T(8,128)(2,1)} %param.21, bf16[256,7168]{1,0:T(8,128)(2,1)} %bitcast.22, bf16[1,7168,256]{2,1,0:T(8,128)(2,1)} %param.20, f32[256,256]{1,0:T(8,128)S(1)} %fusion.17), kind=kOutput, calls=%fused_computation.19 | convolution fusion | flops 1879441408 | bytes 14942208 | tf_op jit(solution)/shard_map/dot_general | solution.py:52
  314.3 15.4 %conditional.1 = (bf16[256,7168]{1,0:T(8,128)(2,1)}) conditional(s32[]{:T(128)} %convert_element_type.141, bf16[256,7168]{1,0:T(8,128)(2,1)} %fusion.11, (s32[16,1,16]{2,1,0:T(1,128)S(1)}, bf16[256,7168]{1,0:T(8,128)(2,1)}, bf16[7168,256]{1,0:T(8,128)(2,1)}, bf16[7168,256]{1,0:T(8,128)(2,1)}, bf16[256,7168]{1,0:T(8,128)(2,1)}, ...), branch_computations={%region_21.22_spmd, %region_22.23_spmd} | conditional | flops 2820800768 | bytes 26216456 | solution.py:119
  314.3 4.3 fusion.66
  318.7 11.1 %convolution_select_fusion = bf16[256,7168]{1,0:T(8,128)(2,1)} fusion(bf16[256,7168]{1,0:T(8,128)(2,1)} %get-tuple-element.27, bf16[256,7168]{1,0:T(8,128)(2,1)} %get-tuple-element.26, pred[256]{0:T(512)(128)(4,1)S(1)} %gt.14, bf16[256,7168]{1,0:T(8,128)(2,1)} %get-tuple-element.23, bf16[7168,256]{1,0:T(8,128)(2,1)} %get-tuple-element.25, ...), kind=kOutput, calls=%fused_computation | convolution fusion | flops 1881276416 | bytes 18612480 | tf_op jit(solution)/shard_map/cond/branch_1_fun/dot_general | solution.py:52
  329.7 46.4 %all_to_all.30 = bf16[16,16,7168]{2,1,0:T(8,128)(2,1)S(1)} all-to-all(bf16[16,16,7168]{2,1,0:T(8,128)(2,1)} %bitcast.91), channel_id=1, replica_groups=mesh['ep'=16,'wide'=8] {'ep'}, dimensions={0} | all-to-all | bytes 7340032 | tf_op jit(solution)/shard_map/all_to_all | solution.py:121
  376.1 3.8 copy.120
  380.0 0.1 reduce_sum.131
  380.1 0.1 reduce_sum.133
  380.4 0.2 copy-done.10
  380.6 0.1 copy.122
  380.7 20.3 %all-gather.1 = bf16[1,64,2]{2,0,1:T(2,128)(2,1)S(1)} all-gather(bf16[1,8,2]{2,0,1:T(2,128)(2,1)S(1)} %copy.122), channel_id=3, replica_groups=mesh['ep'=16,'wide'=8] {'wide'}, dimensions={1}, use_global_device_ids=true | all-gather | bytes 288 | tf_op jit(solution)/shard_map/all_gather | solution.py:81
  401.2 2.9 fusion.8
  404.2 0.1 reduce_sum.140
  404.3 0.1 reduce_sum.142
  404.6 0.1 copy.125
  404.7 12.8 %all-gather.4 = bf16[1,64,2]{2,0,1:T(2,128)(2,1)S(1)} all-gather(bf16[1,8,2]{2,0,1:T(2,128)(2,1)S(1)} %copy.125), channel_id=6, replica_groups=mesh['ep'=16,'wide'=8] {'wide'}, dimensions={1}, use_global_device_ids=true | all-gather | bytes 288 | tf_op jit(solution)/shard_map/all_gather | solution.py:81
  417.7 0.3 reduce-scatter.9.cloned.1.call-done
  418.0 2.9 fusion.9
  420.9 30.0 %reduce-scatter.7.cloned.1.call-done = bf16[8,7168]{1,0:T(8,128)(2,1)} async-done(((bf16[64,7168]{1,0:T(8,128)(2,1)}), bf16[8,7168]{1,0:T(8,128)(2,1)}) %reduce-scatter.7.cloned.1.call-update) | async-done | bytes 114704 | tf_op jit(solution)/shard_map/reduce_scatter | solution.py:136
  450.9 32.9 %reduce-scatter.11.cloned.1.call-done = bf16[8,7168]{1,0:T(8,128)(2,1)} async-done(((bf16[64,7168]{1,0:T(8,128)(2,1)}), bf16[8,7168]{1,0:T(8,128)(2,1)}) %reduce-scatter.11.cloned.1.call-update) | async-done | bytes 114704 | tf_op jit(solution)/shard_map/reduce_scatter | solution.py:136
  483.8 1.7 pad_maximum_fusion
  (74 shorter events, 2.3 us)
Async XLA Ops:
  7.4 306.9 %all-reduce.3.cloned.1.call-start = ((), (), s32[]{:S(2)}) async-start(), calls=%async_computation.13 | async-start | bytes 22020096 | tf_op jit(solution)/shard_map/psum | solution.py:12
  10.0 4.3 copy-start.1
  10.0 5.6 %copy-start.3 = (bf16[1,7168,256]{2,1,0:T(8,128)(2,1)S(1)}, bf16[1,7168,256]{2,1,0:T(8,128)(2,1)}, u32[]{:S(2)}) copy-start(bf16[1,7168,256]{2,1,0:T(8,128)(2,1)} %param.19) | copy-start | bytes 11010052
  19.0 0.7 copy-start.6
  19.0 2.1 copy-start.8
  19.0 15.3 %copy-start.7 = (s32[2,8,2]{1,2,0:T(2,128)S(1)}, s32[2,8,2]{1,2,0:T(2,128)}, u32[]{:S(2)}) copy-start(s32[2,8,2]{1,2,0:T(2,128)} %param.13) | copy-start | bytes 388
  19.0 42.0 %copy-start.11 = (s32[16]{0:T(128)S(1)}, s32[16]{0:T(128)}, u32[]{:S(2)}) copy-start(s32[16]{0:T(128)} %param.16) | copy-start | bytes 196
  19.0 43.2 %copy-start.9 = (s32[2,16]{1,0:T(2,128)S(1)}, s32[2,16]{1,0:T(2,128)}, u32[]{:S(2)}) copy-start(s32[2,16]{1,0:T(2,128)} %param.18) | copy-start | bytes 388
  19.6 44.0 %copy-start.5 = (bf16[2,8,7168]{2,1,0:T(8,128)(2,1)S(1)}, bf16[2,8,7168]{2,1,0:T(8,128)(2,1)}, u32[]{:S(2)}) copy-start(bf16[2,8,7168]{2,1,0:T(8,128)(2,1)} %param.12) | copy-start | bytes 688132
  78.4 62.8 %copy-start.4 = (bf16[1,7168,256]{2,1,0:T(8,128)(2,1)S(1)}, bf16[1,7168,256]{2,1,0:T(8,128)(2,1)}, u32[]{:S(2)}) copy-start(bf16[1,7168,256]{2,1,0:T(8,128)(2,1)} %param.19) | copy-start | bytes 11010052
  141.2 2.0 copy-start.2
  143.2 2.0 copy-start
  150.3 65.7 %all-to-all-start.1 = ((bf16[16,16,7168]{2,1,0:T(8,128)(2,1)}), bf16[16,16,7168]{2,1,0:T(8,128)(2,1)}, u32[]{:S(2)}, u32[]{:S(2)}) async-start(bf16[16,16,7168]{2,1,0:T(8,128)(2,1)} %copy.107), calls=%async_computation.1 | async-start | bytes 7340032 | tf_op jit(solution)/shard_map/all_to_all | solution.py:121
  216.0 79.9 %all-to-all-start.2 = ((bf16[16,16,7168]{2,1,0:T(8,128)(2,1)}), bf16[16,16,7168]{2,1,0:T(8,128)(2,1)}, u32[]{:S(2)}, u32[]{:S(2)}) async-start(bf16[16,16,7168]{2,1,0:T(8,128)(2,1)} %bitcast.92), calls=%async_computation.4 | async-start | bytes 7340032 | tf_op jit(solution)/shard_map/all_to_all | solution.py:108
  221.1 180.1 %reduce-scatter.5.cloned.1.call-start = ((), (), s32[]{:S(2)}) async-start(), calls=%async_computation.9 | async-start | bytes 4128768 | tf_op jit(solution)/shard_map/reduce_scatter | solution.py:124
  296.0 18.3 %all-to-all-start.3 = ((s32[16,1,16]{2,1,0:T(1,128)}), s32[16,1,16]{2,1,0:T(1,128)S(1)}, u32[]{:S(2)}, u32[]{:S(2)}) async-start(s32[16,1,16]{2,1,0:T(1,128)} %bitcast.23), calls=%async_computation.5 | async-start | bytes 16384 | tf_op jit(solution)/shard_map/all_to_all | solution.py:109
  299.9 118.1 %reduce-scatter.9.cloned.1.call-start = ((), (), s32[]{:S(2)}) async-start(), calls=%async_computation.11 | async-start | bytes 4128768 | tf_op jit(solution)/shard_map/reduce_scatter | solution.py:124
  379.9 0.7 copy-start.10
  379.9 71.0 %reduce-scatter.7.cloned.1.call-start = ((), (), s32[]{:S(2)}) async-start(), calls=%async_computation.10 | async-start | bytes 1032192 | tf_op jit(solution)/shard_map/reduce_scatter | solution.py:136
  404.1 79.7 %reduce-scatter.11.cloned.1.call-start = ((), (), s32[]{:S(2)}) async-start(), calls=%async_computation.12 | async-start | bytes 1032192 | tf_op jit(solution)/shard_map/reduce_scatter | solution.py:136
Sparse Core Ops, SparseCore 0:
  19.1 280.3 all-reduce.2
Sparse Core Ops, SparseCore 1:
  227.3 38.2 reduce-scatter.4
  380.0 37.9 reduce-scatter.8
  420.3 30.6 reduce-scatter.6
  453.5 30.3 reduce-scatter.10
where the time goes:
time: 496 us; the launch traced here: 493 us
  blocking collectives  210 us (42%)
  waiting for transfers between devices  172 us (35%)
  matrix products  42.8 us (9%)
  local copies, waits for them, and re-layouts  21.1 us (4%)
  other arithmetic  16.7 us (3%)
  between operations  16.7 us (3%)
  starting transfers between devices  14 us (3%)
    all_to_all x1, waiting for transfers between devices, shards(): lax.all_to_all(outgoing, 'ep', split_axis=0, concat_axis=0, tiled=True)  68.1 us
    reduce_scatter x2, waiting for transfers between devices, shards(): lax.psum_scatter(row_terms.astype(jnp.bfloat16), 'wide', scatter_dimensio...  62.9 us
    all_to_all x1, blocking collectives, shards(): lax.all_to_all(outgoing, 'ep', split_axis=0, concat_axis=0, tiled=True)  62.7 us
    all_to_all x1, blocking collectives, shards(): lax.all_to_all(partial_out.astype(jnp.bfloat16), 'ep', split_axis=0, conc...  46.4 us
    all_to_all x1, waiting for transfers between devices, shards(): lax.all_to_all(partial_out.astype(jnp.bfloat16), 'ep', split_axis=0, conc...  40.9 us
    all_gather x2, blocking collectives, shards(): lax.all_gather(gates[step_index], 'wide', axis=0, tiled=True)  33.1 us
    all_gather x2, blocking collectives, shards(): lax.all_gather(requests[step_index], 'wide', axis=0, tiled=True)  28.6 us
    all_gather x2, blocking collectives, shards(): lax.all_gather(routes[step_index], 'wide', axis=0, tiled=True)  25.6 us
  transfers between devices with their start and end apart: 8, of which 5 were waited for; matrix products, arithmetic and copies ran while one was open for 13% of the time, Pallas kernels for 0%

commit v1 on v0

v1 whole, which is shorter than its diff:
```python
import functools

import jax
import jax.numpy as jnp
import numpy as np
from jax import lax
from jax.experimental import pallas as pl
from jax.experimental.pallas import tpu as pltpu
from jax.sharding import PartitionSpec as P

BF = jnp.bfloat16
F32 = jnp.float32
STEPS = 2
CAP = 16
NE = 16
NW = 8
GROUP = 64
D = 7168
COLS = D // NW
SLOTS = NE * CAP
HALF = SLOTS // 2
HID = 256

STEP_XY = ((1, 0), (-1, 0), (0, 1), (0, -1))
TREES = (
    ((0, 0, 0), (1, 0, 2), (1, 0, 0), (1, 1, 2), (2, 0, 0), (2, 0, 3), (1, 2, 1), (2, 3, 0)),
    ((0, 0, 1), (3, 0, 1), (3, 0, 3), (2, 0, 2), (2, 0, 1), (3, 3, 3), (2, 1, 1), (3, 2, 0)),
    ((0, 0, 2), (0, 1, 1), (0, 1, 0), (0, 1, 2), (3, 1, 3), (1, 1, 3), (3, 1, 2), (3, 2, 2)),
    ((0, 0, 3), (0, 3, 3), (0, 3, 1), (0, 3, 0), (0, 2, 0), (3, 3, 2), (1, 3, 2), (1, 2, 3)),
)
LAG = 2
CHUNKS = 42
T_SLOTS = CHUNKS + 3 * LAG
STAGE = 3


def relay_tables():
    flags = np.zeros((16, 4, 4), np.float32)
    arrive = np.zeros((16, 8), np.int32)
    for tree, edges in enumerate(TREES):
        came = {(0, 0): (None, 0)}
        for x, y, link in edges:
            via, depth = came[(x, y)]
            to = ((x + STEP_XY[link][0]) % 4, (y + STEP_XY[link][1]) % 4)
            assert to not in came
            came[to] = (link, depth + 1)
            place = y * 4 + x
            column = link ^ 1 if via is None else via
            assert flags[place, link].sum() == 0 and (via is None or via != link ^ 1)
            flags[place, link, column] = 1
            arrive[to[1] * 4 + to[0], 2 * tree] = link
            arrive[to[1] * 4 + to[0], 2 * tree + 1] = LAG * depth
    return flags.reshape(16, 16), arrive


FLAGS, ARRIVE = relay_tables()


def rcopy(src, dst, ssem, rsem, dev):
    return pltpu.make_async_remote_copy(
        src_ref=src,
        dst_ref=dst,
        send_sem=ssem,
        recv_sem=rsem,
        device_id=dev,
        device_id_type=pl.DeviceIdType.MESH,
    )


def lanes(start, size):
    return pl.ds(pl.multiple_of(start, 128), size)


def rows16(start, size):
    return pl.ds(pl.multiple_of(start, 16), size)


def layer_kernel(
    req, meta, par, flag, tab, gate, up, down, out,
    xin, xmeta, outg, tgo, tgi, rows, hw, rb, sb, mk, acc, hid, part, sibr, zs, za, zb, rp, rm,
    eo, ret, wc, outb, fin,
    load_sem, x_ss, x_rs, m_ss, m_rs, a_ss, a_rs, t_ss, t_rs, own_sem,
    b_ss, b_rs, gz_ss, gz_rs, gs_ss, gs_rs, s_ss, s_rs, z_ss, z_rs, r_ss, r_rs, f_ss, f_rs,
):
    e = lax.axis_index("ep")
    w = lax.axis_index("wide")
    ex, ey = e % 4, e // 4
    z, c = w // 2, w % 2

    def wide_dev(other):
        return {"ep": e, "wide": other}

    def ep_dev(other):
        return {"ep": other, "wide": w}

    def z_dev(shift):
        return wide_dev(((z + shift) % 4) * 2 + c)

    sibling = wide_dev(z * 2 + 1 - c)
    link_dev = [
        ep_dev(((ey + dy + 4) % 4) * 4 + (ex + dx + 4) % 4) for dx, dy in STEP_XY
    ]

    loads = [
        pltpu.make_async_copy(gate, hw.at[pl.ds(0, 56)], load_sem.at[0]),
        pltpu.make_async_copy(up, hw.at[pl.ds(56, 56)], load_sem.at[1]),
    ]
    for load in loads:
        load.start()

    def load_down(j, carry):
        for half in range(2):
            pltpu.make_async_copy(
                down.at[pl.ds(half * 128, 128), lanes(j * 256, 256)],
                hw.at[112 + 2 * j + half],
                load_sem.at[2],
            ).start()
        return carry

    lax.fori_loop(0, 28, load_down, 0)

    barrier = pltpu.get_barrier_semaphore()
    for j in range(1, NW):
        pl.semaphore_signal(barrier, inc=1, device_id=wide_dev((w + j) % NW), device_id_type=pl.DeviceIdType.MESH)
    for j in range(1, NE):
        pl.semaphore_signal(barrier, inc=1, device_id=ep_dev((e + j) % NE), device_id_type=pl.DeviceIdType.MESH)
    pl.semaphore_wait(barrier, NW - 1 + NE - 1)

    def exchange(j):
        peer = (w + j) % NW
        frm = (w + NW - j) % NW
        return (
            rcopy(req.at[:, lanes(peer * COLS, COLS)], xin.at[w], x_ss.at[j - 1], x_rs.at[j - 1], wide_dev(peer)),
            rcopy(meta, xmeta.at[w], m_ss.at[j - 1], m_rs.at[j - 1], wide_dev(peer)),
            rcopy(req.at[:, lanes(peer * COLS, COLS)], xin.at[frm], x_ss.at[j - 1], x_rs.at[j - 1], wide_dev(peer)),
            rcopy(meta, xmeta.at[frm], m_ss.at[j - 1], m_rs.at[j - 1], wide_dev(peer)),
        )

    for j in range(1, NW):
        copies = exchange(j)
        copies[1].start()
        copies[0].start()
    xin[w] = req[:, lanes(w * COLS, COLS)]
    xmeta[w] = meta[...]

    for link in range(4):
        for k in range(4):
            mk[link * 4 + k] = jnp.full((16, 256), flag[link * 4 + k], F32).astype(BF)

    for load in loads:
        load.wait()
    pltpu.make_async_copy(hw.at[pl.ds(112, 56)], hw.at[pl.ds(112, 56)], load_sem.at[2]).wait()

    def slot_copy(link, t):
        return rcopy(sb.at[link, t % STAGE], rb.at[link, t], b_ss.at[link, t % STAGE], b_rs.at[link, t], link_dev[link])

    def slot(t, with_own, with_recv, with_wait):
        if with_recv:
            for link in range(4):
                slot_copy(link, t - LAG).wait_recv()
        for link in range(4):
            if with_wait:
                slot_copy(link, t - STAGE).wait_send()
            total = None
            for k in range(4):
                if k == link ^ 1:
                    if not with_own:
                        continue
                    block = hw[link * CHUNKS + t]
                else:
                    if not with_recv:
                        continue
                    block = rb[k, t - LAG]
                term = block.reshape(8, 16, 256) * mk[link * 4 + k][None]
                total = term if total is None else total + term
            sb[link, t % STAGE] = total.reshape(128, 256)
            slot_copy(link, t).start()

    cursor = [0]

    def run_slots(count):
        t0 = cursor[0]
        t1 = min(T_SLOTS, t0 + count)
        cursor[0] = t1
        cuts = sorted({t0, t1, *[x for x in (LAG, STAGE, CHUNKS) if t0 < x < t1]})
        for lo, hi in zip(cuts[:-1], cuts[1:]):
            kind = (lo < CHUNKS, lo >= LAG, lo >= STAGE)
            if hi - lo == 1:
                slot(lo, *kind)
            else:
                def body(t, carry, kind=kind):
                    slot(t, *kind)
                    return carry

                lax.fori_loop(lo, hi, body, 0)

    def finish_slots():
        run_slots(T_SLOTS)

        def drain_recv(t, carry):
            for link in range(4):
                slot_copy(link, t).wait_recv()
            return carry

        def drain_send(t, carry):
            for link in range(4):
                slot_copy(link, t).wait_send()
            return carry

        lax.fori_loop(T_SLOTS - LAG, T_SLOTS, drain_recv, 0)
        lax.fori_loop(T_SLOTS - STAGE, T_SLOTS, drain_send, 0)

    def make_plan():
        picks = xmeta[...].reshape(128, 128)
        lane = lax.broadcasted_iota(jnp.int32, (128, 128), 1)
        line = lax.broadcasted_iota(jnp.int32, (128, 128), 0)
        lane_f = lane.astype(F32)
        second = (line // 8) % 2 == 1
        limits = jnp.where(second, jnp.broadcast_to(par[3:4, :], (128, 128)), jnp.broadcast_to(par[2:3, :], (128, 128)))
        place = jnp.broadcast_to(par[0:1, :], (128, 128))
        cand = jnp.broadcast_to(par[1:2, :], (128, 128))
        hot = jnp.broadcast_to(par[4:5, :], (128, 128))
        zero = jnp.zeros((128, 128), F32)

        def spread(column):
            return jnp.broadcast_to(picks[:, column : column + 1], (128, 128))

        def total(v):
            return jnp.broadcast_to(jnp.sum(v, axis=1, keepdims=True), (128, 128))

        onehots, servers, copied = [], [], []
        for k in range(2):
            route, pick = spread(k), spread(2 + k)
            server = total(jnp.where(lane_f == route, place, zero))
            chosen = total(jnp.where(lane_f == pick, cand, zero))
            is_hot = jnp.where(second, jnp.where(route == hot, 1.0, 0.0), 0.0)
            server = jnp.where(is_hot > 0.5, chosen, server)
            copied.append(jnp.where(pick > 0.5, is_hot, 0.0))
            servers.append(server)
            onehots.append(jnp.where(lane_f == server, 1.0, 0.0))
        earlier = jnp.where(lane < line, 1.0, 0.0) * jnp.where((line // 8) % 2 == (lane // 8) % 2, 1.0, 0.0)
        before = jnp.dot(earlier.astype(BF), (onehots[0] + onehots[1]).astype(BF), preferred_element_type=F32)
        lane_w = lax.broadcasted_iota(jnp.int32, (128, 512), 1).astype(F32)
        base = jnp.where(second, float(SLOTS), 0.0)
        matches = []
        for k in range(2):
            count = before if k == 0 else before + onehots[0]
            position = total(count * onehots[k])
            limit = total(limits * onehots[k])
            column = jnp.where(position < limit, base + servers[k] * CAP + position, -1.0)
            matches.append(jnp.where(lane_w == jnp.broadcast_to(column[:, :1], (128, 512)), 1.0, 0.0))

        def wide512(v):
            return jnp.broadcast_to(v[:, :1], (128, 512))

        wc[...] = (matches[0] * wide512(spread(4)) + matches[1] * wide512(spread(5))).astype(BF)
        dispatch = (matches[0] + matches[1]).astype(BF)
        tags = (matches[0] * wide512(copied[0]) + matches[1] * wide512(copied[1])).astype(BF)
        flat = xin[...].reshape(128, COLS)
        contract = (((0,), (0,)), ((), ()))
        for s in range(STEPS):
            outg[s] = lax.dot_general(
                dispatch[:, s * SLOTS : (s + 1) * SLOTS], flat, contract, preferred_element_type=F32
            ).astype(BF)
        tgo[...] = lax.dot_general(
            tags[:, SLOTS:], jnp.ones((128, 128), BF), contract, preferred_element_type=F32
        ).astype(BF)

    def a2a_start(s):
        def send(j, carry):
            peer = (e + j) % NE
            rcopy(
                outg.at[s, rows16(peer * CAP, CAP)], rows.at[s, rows16(e * CAP, CAP), lanes(w * COLS, COLS)],
                a_ss.at[s], a_rs.at[s], ep_dev(peer),
            ).start()
            if s == 1:
                rcopy(
                    tgo.at[rows16(peer * CAP, CAP)], tgi.at[rows16(e * CAP, CAP)], t_ss, t_rs, ep_dev(peer)
                ).start()
            return carry

        lax.fori_loop(1, NE, send, 0)
        rows[s, rows16(e * CAP, CAP), lanes(w * COLS, COLS)] = outg[s, rows16(e * CAP, CAP), :]
        if s == 1:
            tgi[rows16(e * CAP, CAP), :] = tgo[rows16(e * CAP, CAP), :]

    def a2a_wait(s):
        n = (NE - 1) * CAP
        done = rcopy(
            outg.at[s, pl.ds(0, n)], rows.at[s, pl.ds(0, n), lanes(w * COLS, COLS)], a_ss.at[s], a_rs.at[s],
            ep_dev((e + 1) % NE),
        )
        done.wait_recv()
        done.wait_send()
        if s == 1:
            done = rcopy(tgo.at[pl.ds(0, n)], tgi.at[pl.ds(0, n)], t_ss, t_rs, ep_dev((e + 1) % NE))
            done.wait_recv()
            done.wait_send()

    def shard(s, shift, core, half):
        col = (((z + shift + 4) % 4) * 2 + core) * COLS
        lo, n = (0, SLOTS) if half is None else (half * HALF, HALF)
        return rows.at[s, pl.ds(lo, n), lanes(col, COLS)]

    GZ = ((1, 0, 0), (1, 0, 1), (-1, 0, 1), (-1, 0, 0), (1, -1, 0), (-1, 1, 1))

    def gz_send(s, k):
        direction, shift, half = GZ[k]
        src = shard(s, shift, c, half)
        return rcopy(src, src, gz_ss.at[s, k], gz_rs.at[s, k], z_dev(direction + 4))

    def gz_wait(s, k):
        direction, shift, half = GZ[k]
        ref = shard(s, shift - direction, c, half)
        rcopy(ref, ref, gz_ss.at[s, k], gz_rs.at[s, k], z_dev(direction + 4)).wait_recv()

    GS = ((0, None), (-1, 0), (1, 1), (-1, 1), (1, 0), (2, 0), (2, 1))

    def gs_send(s, k):
        src = shard(s, GS[k][0], c, GS[k][1])
        return rcopy(src, src, gs_ss.at[s, k], gs_rs.at[s, k], sibling)

    def gs_wait(s, k):
        ref = shard(s, GS[k][0], 1 - c, GS[k][1])
        rcopy(ref, ref, gs_ss.at[s, k], gs_rs.at[s, k], sibling).wait_recv()

    def gather0(s):
        for k in (0, 2, 1, 3):
            gz_send(s, k).start()
        gs_send(s, 0).start()

    def gather1(s):
        gz_wait(s, 0)
        gz_send(s, 4).start()
        gs_send(s, 1).start()
        gz_wait(s, 2)
        gz_send(s, 5).start()
        gs_send(s, 2).start()

    def gather2(s):
        gz_wait(s, 1)
        gs_send(s, 3).start()
        gz_wait(s, 3)
        gs_send(s, 4).start()

    def gather3(s):
        gz_wait(s, 4)
        gs_send(s, 5).start()
        gz_wait(s, 5)
        gs_send(s, 6).start()

    def gather4(s):
        for k in range(7):
            gs_wait(s, k)

    def gather_drain(s):
        for k in range(6):
            gz_send(s, k).wait_send()
        for k in range(7):
            gs_send(s, k).wait_send()

    def silu_mul():
        g = acc[0]
        return g / (1.0 + jnp.exp(-g)) * acc[1]

    def hidden_home(s):
        acc[...] = jnp.zeros_like(acc)

        def body(k, carry):
            x = rows[s, :, lanes(k * 1024, 1024)]
            acc[0] += jnp.dot(x, hw[pl.ds(k * 8, 8)].reshape(1024, 256), preferred_element_type=F32)
            acc[1] += jnp.dot(x, hw[pl.ds(56 + k * 8, 8)].reshape(1024, 256), preferred_element_type=F32)
            return carry

        lax.fori_loop(0, 7, body, 0)
        h = silu_mul()
        if s == 1:
            tag = tgi[...].astype(F32)
            h = h * (1.0 - jnp.concatenate([tag, tag], axis=1))
        hid[s] = h.astype(BF)

    def hidden_copy():
        acc[...] = jnp.zeros_like(acc)
        for dest, first, last in ((0, 0, 21), (0, 21, 28), (1, 28, 42), (1, 42, 56)):
            tree = first // 21

            def body(b, carry, dest=dest, tree=tree):
                x = rows[1, :, lanes((b - 28 * dest) * 256, 256)]
                block = rb[tab[2 * tree], pl.ds(2 * (b - 21 * tree) + tab[2 * tree + 1], 2)]
                acc[dest] += jnp.dot(x, block.reshape(256, 256), preferred_element_type=F32)
                return carry

            lax.fori_loop(first, last, body, 0)
        tag = tgi[...].astype(F32)
        hid[2] = (silu_mul() * jnp.concatenate([tag, tag], axis=1)).astype(BF)

    def block_cols(s, zi, core):
        return lanes((((z + zi) % 4) * 2 + core) * COLS, COLS)

    def sib_copy(s, zi):
        return rcopy(part.at[s, :, block_cols(s, zi, 1 - c)], sibr.at[s, zi], s_ss.at[s, zi], s_rs.at[s, zi], sibling)

    def partials(s):
        for zi in (2, 1, 3, 0):
            zz = (z + zi) % 4

            def body(jj, carry, zz=zz):
                j = zz * 7 + jj
                v = jnp.dot(hid[s], hw[pl.ds(112 + 2 * j, 2)].reshape(256, 256), preferred_element_type=F32)
                if s == 1:
                    first = zz == 0
                    link = jnp.where(first, tab[4], tab[6])
                    t = jnp.where(first, 28 + tab[5], (zz - 1) * 14 + tab[7]) + 2 * jj
                    block = rb[link, pl.ds(t, 2)]
                    v += jnp.dot(hid[2], block.reshape(256, 256), preferred_element_type=F32)
                part[s, :, lanes(j * 256, 256)] = v.astype(BF)
                return carry

            lax.fori_loop(0, 7, body, 0)
            sib_copy(s, zi).start()

    def pair_sum(s, zi):
        return part[s, :, block_cols(s, zi, c)].astype(F32) + sibr[s, zi].astype(F32)

    lo_half, hi_half = pl.ds(0, HALF), pl.ds(HALF, HALF)

    def z_copy(s, k):
        src, dst, direction = (
            (zs.at[s, 0, lo_half], za.at[s], 1),
            (zs.at[s, 0, hi_half], zb.at[s], -1),
            (zs.at[s, 1, hi_half], rp.at[s, hi_half], 1),
            (zs.at[s, 1, lo_half], rp.at[s, lo_half], 1),
            (zs.at[s, 2, lo_half], rm.at[s, lo_half], -1),
            (zs.at[s, 2, hi_half], rm.at[s, hi_half], -1),
        )[k]
        return rcopy(src, dst, z_ss.at[s, k], z_rs.at[s, k], z_dev(direction + 4))

    def reduce1(s):
        sib_copy(s, 2).wait_recv()
        zs[s, 0] = pair_sum(s, 2).astype(BF)
        z_copy(s, 0).start()
        z_copy(s, 1).start()
        sib_copy(s, 1).wait_recv()
        zs[s, 1] = pair_sum(s, 1).astype(BF)
        z_copy(s, 2).start()
        sib_copy(s, 3).wait_recv()
        zs[s, 2] = pair_sum(s, 3).astype(BF)
        z_copy(s, 4).start()

    def reduce2(s):
        z_copy(s, 0).wait_recv()
        zs[s, 1, lo_half] = (zs[s, 1, lo_half].astype(F32) + za[s].astype(F32)).astype(BF)
        z_copy(s, 3).start()
        z_copy(s, 1).wait_recv()
        zs[s, 2, hi_half] = (zs[s, 2, hi_half].astype(F32) + zb[s].astype(F32)).astype(BF)
        z_copy(s, 5).start()

    def reduce3(s):
        sib_copy(s, 0).wait_recv()
        for k in (2, 4, 3, 5):
            z_copy(s, k).wait_recv()
        eo[s] = (pair_sum(s, 0) + rp[s].astype(F32) + rm[s].astype(F32)).astype(BF)

    def reduce_drain(s):
        for zi in range(4):
            sib_copy(s, zi).wait_send()
        for k in range(6):
            z_copy(s, k).wait_send()

    def back_start(s):
        def send(j, carry):
            peer = (e + j) % NE
            rcopy(
                eo.at[s, rows16(peer * CAP, CAP)], ret.at[rows16(s * SLOTS + e * CAP, CAP)],
                r_ss.at[s], r_rs.at[s], ep_dev(peer),
            ).start()
            return carry

        lax.fori_loop(1, NE, send, 0)
        ret[rows16(s * SLOTS + e * CAP, CAP), :] = eo[s, rows16(e * CAP, CAP), :]

    def back_wait(s):
        n = (NE - 1) * CAP
        done = rcopy(
            eo.at[s, pl.ds(0, n)], ret.at[pl.ds(s * SLOTS, n)], r_ss.at[s], r_rs.at[s], ep_dev((e + 1) % NE)
        )
        done.wait_recv()
        done.wait_send()

    def final(j):
        peer = (w + j) % NW
        frm = (w + NW - j) % NW
        return (
            rcopy(outb.at[rows16(peer * 16, 16)], fin.at[w], f_ss.at[j - 1], f_rs.at[j - 1], wide_dev(peer)),
            rcopy(outb.at[rows16(peer * 16, 16)], fin.at[frm], f_ss.at[j - 1], f_rs.at[j - 1], wide_dev(peer)),
        )

    run_slots(2)
    for j in range(1, NW):
        copies = exchange(j)
        copies[2].wait_recv()
        copies[3].wait_recv()
    make_plan()
    a2a_start(0)
    a2a_start(1)
    run_slots(4)
    a2a_wait(0)
    gather0(0)
    run_slots(4)
    gather1(0)
    a2a_wait(1)
    run_slots(3)
    gather2(0)
    gather0(1)
    run_slots(3)
    gather3(0)
    run_slots(1)
    gather4(0)
    hidden_home(0)
    run_slots(2)
    gather1(1)
    partials(0)
    run_slots(2)
    gather2(1)
    reduce1(0)
    run_slots(2)
    gather3(1)
    run_slots(2)
    reduce2(0)
    gather4(1)
    run_slots(2)
    hidden_home(1)
    run_slots(4)
    reduce3(0)
    back_start(0)
    finish_slots()
    hidden_copy()
    partials(1)
    reduce1(1)
    back_wait(0)
    reduce2(1)
    reduce3(1)
    back_start(1)
    back_wait(1)
    outb[...] = jnp.dot(wc[...], ret[...], preferred_element_type=F32).astype(BF)
    for j in range(1, NW):
        final(j)[0].start()
    fin[w] = outb[rows16(w * 16, 16), :]
    for j in range(1, NW):
        copies = exchange(j)
        copies[0].wait_send()
        copies[1].wait_send()
    for s in range(STEPS):
        gather_drain(s)
        reduce_drain(s)
    for j in range(1, NW):
        final(j)[1].wait_recv()
    for k in range(NW):
        out[:, k * COLS : (k + 1) * COLS] = fin[k]
    for j in range(1, NW):
        final(j)[0].wait_send()


def shards(
    requests, routes, gates, replica, placement, copy_plan, capacity, gate_proj, up_proj, down_proj
):
    e = lax.axis_index("ep")
    own = requests.shape[1]
    req = requests.reshape(STEPS * own, D)
    slots = jnp.arange(NE, dtype=jnp.int32)
    home = jnp.sum(jnp.where(slots == copy_plan[0], placement, 0), dtype=jnp.int32)
    cand = (home + jnp.concatenate([jnp.zeros((1,), jnp.int32), copy_plan[1:]])) % NE
    picks = jnp.concatenate(
        [
            routes.astype(F32),
            jnp.broadcast_to(replica.astype(F32)[None], routes.shape),
            gates.astype(F32),
        ],
        axis=2,
    ).reshape(STEPS * own, 6)
    meta = jnp.pad(picks, ((0, 0), (0, 122)))
    par = jnp.concatenate(
        [
            jnp.pad(placement[None].astype(F32), ((0, 0), (0, 112))),
            jnp.pad(cand[None].astype(F32), ((0, 0), (0, 124))),
            jnp.pad(capacity.astype(F32), ((0, 0), (0, 112))),
            jnp.broadcast_to(copy_plan[:1].astype(F32)[None], (1, 128)),
            jnp.zeros((3, 128), F32),
        ],
        axis=0,
    )
    place = ((e // 4 - home // 4) % 4) * 4 + (e % 4 - home % 4) % 4
    at_place = (slots == place)[:, None]
    flag = jnp.sum(jnp.where(at_place, jnp.asarray(FLAGS), 0.0), axis=0)
    tab = jnp.sum(jnp.where(at_place, jnp.asarray(ARRIVE), 0), axis=0, dtype=jnp.int32)

    vmem = pl.BlockSpec(memory_space=pltpu.VMEM)
    smem = pl.BlockSpec(memory_space=pltpu.SMEM)
    hbm = pl.BlockSpec(memory_space=pl.ANY)
    dma = pltpu.SemaphoreType.DMA
    result = pl.pallas_call(
        layer_kernel,
        out_shape=jax.ShapeDtypeStruct((STEPS * own, D), BF),
        in_specs=[vmem, vmem, vmem, smem, smem, hbm, hbm, hbm],
        out_specs=vmem,
        scratch_shapes=[
            pltpu.VMEM((NW, 16, COLS), BF),
            pltpu.VMEM((NW, 16, 128), F32),
            pltpu.VMEM((STEPS, SLOTS, COLS), BF),
            pltpu.VMEM((SLOTS, 128), BF),
            pltpu.VMEM((SLOTS, 128), BF),
            pltpu.VMEM((STEPS, SLOTS, D), BF),
            pltpu.VMEM((168, 128, 256), BF),
            pltpu.VMEM((4, T_SLOTS, 128, 256), BF),
            pltpu.VMEM((4, STAGE, 128, 256), BF),
            pltpu.VMEM((16, 16, 256), BF),
            pltpu.VMEM((2, SLOTS, HID), F32),
            pltpu.VMEM((3, SLOTS, HID), BF),
            pltpu.VMEM((STEPS, SLOTS, D), BF),
            pltpu.VMEM((STEPS, 4, SLOTS, COLS), BF),
            pltpu.VMEM((STEPS, 3, SLOTS, COLS), BF),
            pltpu.VMEM((STEPS, HALF, COLS), BF),
            pltpu.VMEM((STEPS, HALF, COLS), BF),
            pltpu.VMEM((STEPS, SLOTS, COLS), BF),
            pltpu.VMEM((STEPS, SLOTS, COLS), BF),
            pltpu.VMEM((STEPS, SLOTS, COLS), BF),
            pltpu.VMEM((STEPS * SLOTS, COLS), BF),
            pltpu.VMEM((128, STEPS * SLOTS), BF),
            pltpu.VMEM((128, COLS), BF),
            pltpu.VMEM((NW, 16, COLS), BF),
            dma((3,)),
            dma((7,)), dma((7,)), dma((7,)), dma((7,)),
            dma((2,)), dma((2,)), dma, dma, dma,
            dma((4, STAGE)), dma((4, T_SLOTS)),
            dma((2, 6)), dma((2, 6)), dma((2, 7)), dma((2, 7)),
            dma((2, 4)), dma((2, 4)), dma((2, 6)), dma((2, 6)),
            dma((2,)), dma((2,)), dma((7,)), dma((7,)),
        ],
        compiler_params=pltpu.CompilerParams(
            collective_id=0, has_side_effects=True, vmem_limit_bytes=62 * 1024 * 1024
        ),
        name="expert_layer",
    )(
        req, meta, par, flag, tab,
        gate_proj.reshape(56, 128, HID), up_proj.reshape(56, 128, HID), down_proj.reshape(HID, D),
    )
    return result.reshape(STEPS, own, D)


def solution(mesh):
    rows = P(None, ("ep", "wide"), None)
    placed = (
        rows, rows, rows, P(("ep", "wide"), None), P(), P(), P(),
        P("ep", None, "wide"), P("ep", None, "wide"), P("ep", "wide", None),
    )
    return jax.shard_map(shards, mesh=mesh, in_specs=placed, out_specs=rows, check_vma=False)
```

time: 496 us -> 196 us (0.40)
  blocking collectives: 210 us -> 0 us
  Pallas kernels: 0 us -> 181 us
  waiting for transfers between devices: 172 us -> 0 us
  matrix products: 42.8 us -> 0 us
  local copies, waits for them, and re-layouts: 21.1 us -> 3.7 us
  starting transfers between devices: 14 us -> 0 us
  between operations: 16.7 us -> 3.34 us
  other arithmetic: 16.7 us -> 8.18 us
    pallas_call x0 -> x1, Pallas kernels: none -> 181 us  [shards(): pl.pallas_call(layer_kernel, out_shape=jax.ShapeDtypeStruct((STEPS * own,...]
    all_to_all x2 -> x0, blocking collectives: 109 us -> none  [the longest x1 62.7 us: shards(): lax.all_to_all(outgoing, 'ep', split_axis=0, concat_axis=0, tiled=True)]
    all_to_all x3 -> x0, waiting for transfers between devices: 109 us -> none  [the longest x1 68.1 us: shards(): lax.all_to_all(outgoing, 'ep', split_axis=0, concat_axis=0, tiled=True)]
    all_gather x7 -> x0, blocking collectives: 100 us -> none  [the longest x2 33.1 us: shards(): lax.all_gather(gates[step_index], 'wide', axis=0, tiled=True)]
    reduce_scatter x4 -> x0, waiting for transfers between devices: 63.2 us -> none  [the longest x2 62.9 us: shards(): lax.psum_scatter(row_terms.astype(jnp.bfloat16), 'wide', scatter_dimensio...]
    dot_general x11 -> x0, matrix products: 42.8 us -> none  [the longest x3 22.2 us: run_expert(): return jnp.dot(hidden, down_w, preferred_element_type=jnp.float32)]
    all_to_all x3 -> x0, starting transfers between devices: 13.8 us -> none  [the longest x1 5.08 us: shards(): lax.all_to_all(outgoing, 'ep', split_axis=0, concat_axis=0, tiled=True)]
    all_to_all x2 -> x0, local copies, waits for them, and re-layouts: 9.86 us -> none  [shards(): lax.all_to_all(partial_out.astype(jnp.bfloat16), 'ep', split_axis=0, conc...]
  transfers between devices with their start and end apart: 8 -> 0, of which waited for: 5 -> 0; matrix products, arithmetic and copies ran while one was open for 13% -> 0% of each run, Pallas kernels for 0% -> 0%
where the time goes in v1:
time: 196 us
  Pallas kernels  181 us (92%)
  other arithmetic  8.18 us (4%)
  local copies, waits for them, and re-layouts  3.7 us (2%)
  between operations  3.34 us (2%)
    pallas_call x1, Pallas kernels, shards(): pl.pallas_call(layer_kernel, out_shape=jax.ShapeDtypeStruct((STEPS * own,...  181 us

profile of v1, /device:TPU:1, one launch (start us, length us, event | category | flops | bytes accessed | tf_op | source)
XLA Modules:
  0.0 195.8 jit_solution(17774394150128078292)
XLA Ops:
  0.7 0.7 slice_bitcast_fusion
  1.4 0.7 convert_element_type.41
  2.1 0.7 convert_element_type.46
  2.8 2.0 %fusion = (s32[]{:T(128)}, f32[1,16]{1,0:T(1,128)S(1)}) fusion(s32[16]{0:T(128)} %param.16, s32[]{:T(128)} %bitcast.20), kind=kLoop, calls=%fused_computation.7 | loop fusion | flops 63 | bytes 136 | tf_op jit(solution)/shard_map/reduce_sum | solution.py:571
  7.5 0.7 fusion.1
  8.2 1.4 select_reduce_fusion.1.tab
  9.6 1.3 select_reduce_fusion.flag
  10.9 0.7 convert_element_type.40
  11.6 0.7 convert_element_type.42
  12.3 0.1 copy.17
  12.4 0.6 pad.16.meta
  13.0 0.6 concatenate.21.par
  13.6 180.6 %expert_layer.1 = bf16[16,7168]{1,0:T(8,128)(2,1)} custom-call(bf16[16,7168]{1,0:T(8,128)(2,1)} %bitcast.17, f32[16,128]{1,0:T(8,128)} %pad.16.meta, f32[8,128]{1,0:T(8,128)} %concatenate.21.par, f32[16]{0:T(128)} %select_reduce_fusion.flag, s32[8]{0:T(128)} %select_reduce_fusion.1.tab, bf16[56,128,256]{2,1,0:T(8,128)(2,1)} %bitcast.13, ...), custom_call_target="tpu_custom_call" | custom-call | tf_op jit(solution)/shard_map/expert_layer/pallas_call | solution.py:601
  194.2 1.6 copy.20
  (8 shorter events, 0.0 us)

commit v2 on v1

v2 whole, which is shorter than its diff:
```python
import jax
import jax.numpy as jnp
from jax import lax
from jax.experimental import pallas as pl
from jax.experimental.pallas import tpu as pltpu
from jax.sharding import PartitionSpec as P

BF = jnp.bfloat16
F32 = jnp.float32
STEPS = 2
CAP = 16
NE = 16
NW = 8
GROUP = 64
D = 7168
COLS = D // NW
SLOTS = NE * CAP
HALF = SLOTS // 2
HID = 256

TILES = COLS // 128

STEP_XY = ((1, 0), (-1, 0), (0, 1), (0, -1))
TREES = (
    ((0, 0, 0), (1, 0, 2), (1, 0, 0), (1, 1, 2), (2, 0, 0), (2, 0, 3), (1, 2, 1), (2, 3, 0)),
    ((0, 0, 1), (3, 0, 1), (3, 0, 3), (2, 0, 2), (2, 0, 1), (3, 3, 3), (2, 1, 1), (3, 2, 0)),
    ((0, 0, 2), (0, 1, 1), (0, 1, 0), (0, 1, 2), (3, 1, 3), (1, 1, 3), (3, 1, 2), (3, 2, 2)),
    ((0, 0, 3), (0, 3, 3), (0, 3, 1), (0, 3, 0), (0, 2, 0), (3, 3, 2), (1, 3, 2), (1, 2, 3)),
)
LAG = 3
CHUNKS = 42
FIRST = 28
T_SLOTS = CHUNKS + 3 * LAG
T_STEPS = CHUNKS + 4 * LAG
STAGE = 4
RING = 16


def relay_tables():
    relay, arrive = {}, [{} for _ in TREES]
    for tree, edges in enumerate(TREES):
        came = {(0, 0): (None, 0)}
        for x, y, link in edges:
            via, depth = came[(x, y)]
            to = ((x + STEP_XY[link][0]) % 4, (y + STEP_XY[link][1]) % 4)
            came[to] = (link, depth + 1)
            relay.setdefault((link, link ^ 1 if via is None else via), []).append(y * 4 + x)
            if to in OWNERS:
                arrive[tree].setdefault((link, LAG * depth), []).append(to[1] * 4 + to[0])
    return relay, arrive


OWNERS = ((1, 0), (1, 1), (3, 0), (3, 3), (0, 2))
RELAY, ARRIVE = relay_tables()
MASKS = [("relay", key) for key in sorted(RELAY)] + [
    ("arrive", tree, key) for tree in range(4) for key in sorted(ARRIVE[tree])
]
MASK_AT = {name: i for i, name in enumerate(MASKS)}


def rcopy(src, dst, ssem, rsem, dev):
    return pltpu.make_async_remote_copy(
        src_ref=src,
        dst_ref=dst,
        send_sem=ssem,
        recv_sem=rsem,
        device_id=dev,
        device_id_type=pl.DeviceIdType.MESH,
    )


def lanes(start, size):
    return pl.ds(pl.multiple_of(start, 128), size)


def rows16(start, size):
    return pl.ds(pl.multiple_of(start, 16), size)


def layer_kernel(
    req, routes, gates, replica, placement, copy_plan, capacity, gate, up, down, out,
    xs, meta, xin, xmeta, outg, tgo, tgi, rows, hw, hot, rb, sb, mk, acc, hid, part, sibr, zs, za, zb, rp, rm,
    eo, ret, wc, outb, fin,
    load_sem, x_ss, x_rs, m_ss, m_rs, a_ss, a_rs, t_ss, t_rs,
    b_ss, b_rs, gz_ss, gz_rs, gs_ss, gs_rs, s_ss, s_rs, z_ss, z_rs, r_ss, r_rs, f_ss, f_rs,
):
    e = lax.axis_index("ep")
    w = lax.axis_index("wide")
    ex, ey = e % 4, e // 4
    z, c = w // 2, w % 2

    def wide_dev(other):
        return {"ep": e, "wide": other}

    def ep_dev(other):
        return {"ep": other, "wide": w}

    def z_dev(shift):
        return wide_dev(((z + shift) % 4) * 2 + c)

    sibling = wide_dev(z * 2 + 1 - c)
    link_dev = [
        ep_dev(((ey + dy + 4) % 4) * 4 + (ex + dx + 4) % 4) for dx, dy in STEP_XY
    ]

    def load_weights(j, carry):
        for i, ref in enumerate((gate, up)):
            pltpu.make_async_copy(ref.at[:, j], hw.at[pl.ds(56 * i + TILES * j, TILES)], load_sem).start()
        return carry

    lax.fori_loop(0, NW, load_weights, 0)

    def load_down(j, carry):
        for half in range(2):
            pltpu.make_async_copy(
                down.at[pl.ds(half * 128, 128), lanes(j * 256, 256)], hw.at[112 + 2 * j + half], load_sem
            ).start()
        return carry

    lax.fori_loop(0, 28, load_down, 0)

    barrier = pltpu.get_barrier_semaphore()
    for j in range(1, NW):
        pl.semaphore_signal(barrier, inc=1, device_id=wide_dev((w + j) % NW), device_id_type=pl.DeviceIdType.MESH)
    for j in range(1, NE):
        pl.semaphore_signal(barrier, inc=1, device_id=ep_dev((e + j) % NE), device_id_type=pl.DeviceIdType.MESH)

    both = jnp.concatenate([req[0].astype(F32), req[1].astype(F32)], axis=0).astype(BF)
    for k in range(NW):
        for q in range(TILES):
            xs[k, :, q * 128 : (q + 1) * 128] = both[:, q * 1024 + k * 128 : q * 1024 + (k + 1) * 128]
    lane8 = lax.broadcasted_iota(jnp.int32, (8, 128), 1)
    for s in range(STEPS):
        line = jnp.zeros((8, 128), F32)
        for i, ref in enumerate((routes[s], replica[...], gates[s])):
            values = ref.astype(F32)
            for k in range(2):
                line = jnp.where(lane8 == 2 * i + k, jnp.broadcast_to(values[:, k : k + 1], (8, 128)), line)
        meta[s * 8 : (s + 1) * 8, :] = line

    def spread_row(values):
        line = jnp.zeros((8, 128), jnp.int32)
        for i, value in enumerate(values):
            line = jnp.where(lane8 == i, value, line)
        return jnp.broadcast_to(line[0:1, :].astype(F32), (128, 128))

    home = placement[copy_plan[0]]
    place = ((ey - home // 4 + 4) % 4) * 4 + (ex - home % 4 + 4) % 4
    places = jnp.full((16, 256), place, jnp.int32)
    for i, name in enumerate(MASKS):
        mask = jnp.zeros((16, 256), F32)
        for at in RELAY[name[1]] if name[0] == "relay" else ARRIVE[name[1]][name[2]]:
            mask = jnp.where(places == at, 1.0, mask)
        mk[i] = mask.astype(BF)

    pl.semaphore_wait(barrier, NW - 1 + NE - 1)

    def exchange(j, peer, at):
        return (
            rcopy(xs.at[(w + j) % NW], xin.at[at], x_ss.at[j - 1], x_rs.at[j - 1], wide_dev(peer)),
            rcopy(meta, xmeta.at[at], m_ss.at[j - 1], m_rs.at[j - 1], wide_dev(peer)),
        )

    for j in range(1, NW):
        for copy in reversed(exchange(j, (w + j) % NW, w)):
            copy.start()
    xin[w] = xs[w]
    xmeta[w] = meta[...]
    pltpu.make_async_copy(hw, hw, load_sem).wait()

    def slot_copy(link, t):
        return rcopy(
            sb.at[link, t % STAGE], rb.at[link, t % RING], b_ss.at[link, t % STAGE], b_rs.at[link, t % RING],
            link_dev[link],
        )

    def chunk_at(tree, n, later):
        return 112 + ((n - FIRST) // 2 * 4 + tree) * 2 + n % 2 if later else tree * FIRST + n

    def masked(block, mask):
        return block.reshape(8, 16, 256) * mk[MASK_AT[mask]][None]

    def add(total, term):
        return term if total is None else total + term

    def step(t, own, own_later, recv, wait, send, deliver, deliver_later):
        if recv:
            for link in range(4):
                slot_copy(link, t - LAG).wait_recv()
        if send:
            for link in range(4):
                if wait:
                    slot_copy(link, t - STAGE).wait_send()
                total = None
                for k in range(4):
                    if (link, k) not in RELAY:
                        continue
                    if k == link ^ 1:
                        if own:
                            total = add(total, masked(hw[chunk_at(link, t, own_later)], ("relay", (link, k))))
                    elif recv:
                        total = add(total, masked(rb[k, (t - LAG) % RING], ("relay", (link, k))))
                sb[link, t % STAGE] = total.reshape(128, 256)
                slot_copy(link, t).start()
        if deliver:
            n = t - 4 * LAG
            for tree in range(4):
                total = None
                for link, behind in sorted(ARRIVE[tree]):
                    block = rb[link, (n + behind) % RING]
                    total = add(total, masked(block, ("arrive", tree, (link, behind))))
                hot[chunk_at(tree, n, deliver_later)] = total.reshape(128, 256)

    cursor = [0]

    def run_to(t1):
        t0 = cursor[0]
        t1 = max(t0, min(T_STEPS, t1))
        cursor[0] = t1
        marks = (LAG, STAGE, FIRST, CHUNKS, T_SLOTS, 4 * LAG, 4 * LAG + FIRST)
        cuts = sorted({t0, t1, *[x for x in marks if t0 < x < t1]})
        for lo, hi in zip(cuts[:-1], cuts[1:]):
            kind = (
                lo < CHUNKS, lo >= FIRST, lo >= LAG, lo >= STAGE, lo < T_SLOTS, lo >= 4 * LAG, lo >= 4 * LAG + FIRST
            )
            if hi - lo == 1:
                step(lo, *kind)
            else:
                def body(t, carry, kind=kind):
                    step(t, *kind)
                    return carry

                lax.fori_loop(lo, hi, body, 0)

    def run(count):
        run_to(cursor[0] + count)

    def drain_slots():
        def drain_send(t, carry):
            for link in range(4):
                slot_copy(link, t).wait_send()
            return carry

        lax.fori_loop(T_SLOTS - STAGE, T_SLOTS, drain_send, 0)

    def make_plan():
        picks = xmeta[...].reshape(128, 128)
        lane = lax.broadcasted_iota(jnp.int32, (128, 128), 1)
        line = lax.broadcasted_iota(jnp.int32, (128, 128), 0)
        lane_f = lane.astype(F32)
        second = (line // 8) % 2 == 1
        limits = jnp.where(
            second,
            spread_row([capacity[1, i] for i in range(NE)]),
            spread_row([capacity[0, i] for i in range(NE)]),
        )
        slot_of = spread_row([placement[i] for i in range(NE)])
        cand = spread_row([home] + [(home + copy_plan[i]) % NE for i in range(1, 4)])
        hot_id = jnp.full((128, 128), copy_plan[0], jnp.int32).astype(F32)
        zero = jnp.zeros((128, 128), F32)

        def spread(column):
            return jnp.broadcast_to(picks[:, column : column + 1], (128, 128))

        def total(v):
            return jnp.broadcast_to(jnp.sum(v, axis=1, keepdims=True), (128, 128))

        onehots, servers, copied = [], [], []
        for k in range(2):
            route, pick = spread(k), spread(2 + k)
            server = total(jnp.where(lane_f == route, slot_of, zero))
            chosen = total(jnp.where(lane_f == pick, cand, zero))
            is_hot = jnp.where(second, jnp.where(route == hot_id, 1.0, 0.0), 0.0)
            server = jnp.where(is_hot > 0.5, chosen, server)
            copied.append(jnp.where(pick > 0.5, is_hot, 0.0))
            servers.append(server)
            onehots.append(jnp.where(lane_f == server, 1.0, 0.0))
        earlier = jnp.where(lane < line, 1.0, 0.0) * jnp.where((line // 8) % 2 == (lane // 8) % 2, 1.0, 0.0)
        before = jnp.dot(earlier.astype(BF), (onehots[0] + onehots[1]).astype(BF), preferred_element_type=F32)
        lane_w = lax.broadcasted_iota(jnp.int32, (128, 512), 1).astype(F32)
        base = jnp.where(second, float(SLOTS), 0.0)
        matches = []
        for k in range(2):
            count = before if k == 0 else before + onehots[0]
            position = total(count * onehots[k])
            limit = total(limits * onehots[k])
            column = jnp.where(position < limit, base + servers[k] * CAP + position, -1.0)
            matches.append(jnp.where(lane_w == jnp.broadcast_to(column[:, :1], (128, 512)), 1.0, 0.0))

        def wide512(v):
            return jnp.broadcast_to(v[:, :1], (128, 512))

        wc[...] = (matches[0] * wide512(spread(4)) + matches[1] * wide512(spread(5))).astype(BF)
        dispatch = (matches[0] + matches[1]).astype(BF)
        tags = (matches[0] * wide512(copied[0]) + matches[1] * wide512(copied[1])).astype(BF)
        flat = xin[...].reshape(128, COLS)
        contract = (((0,), (0,)), ((), ()))
        for s in range(STEPS):
            outg[s] = lax.dot_general(
                dispatch[:, s * SLOTS : (s + 1) * SLOTS], flat, contract, preferred_element_type=F32
            ).astype(BF)
        tgo[...] = lax.dot_general(
            tags[:, SLOTS:], jnp.ones((128, 128), BF), contract, preferred_element_type=F32
        ).astype(BF)

    def a2a_start(s):
        def send(j, carry):
            peer = (e + j) % NE
            rcopy(
                outg.at[s, rows16(peer * CAP, CAP)], rows.at[s, rows16(e * CAP, CAP), lanes(w * COLS, COLS)],
                a_ss.at[s], a_rs.at[s], ep_dev(peer),
            ).start()
            if s == 1:
                rcopy(
                    tgo.at[rows16(peer * CAP, CAP)], tgi.at[rows16(e * CAP, CAP)], t_ss, t_rs, ep_dev(peer)
                ).start()
            return carry

        lax.fori_loop(1, NE, send, 0)
        rows[s, rows16(e * CAP, CAP), lanes(w * COLS, COLS)] = outg[s, rows16(e * CAP, CAP), :]
        if s == 1:
            tgi[rows16(e * CAP, CAP), :] = tgo[rows16(e * CAP, CAP), :]

    def a2a_wait(s):
        n = (NE - 1) * CAP
        done = rcopy(
            outg.at[s, pl.ds(0, n)], rows.at[s, pl.ds(0, n), lanes(w * COLS, COLS)], a_ss.at[s], a_rs.at[s],
            ep_dev((e + 1) % NE),
        )
        done.wait_recv()
        done.wait_send()
        if s == 1:
            done = rcopy(tgo.at[pl.ds(0, n)], tgi.at[pl.ds(0, n)], t_ss, t_rs, ep_dev((e + 1) % NE))
            done.wait_recv()
            done.wait_send()

    def shard(s, shift, core, half):
        col = (((z + shift + 4) % 4) * 2 + core) * COLS
        lo, n = (0, SLOTS) if half is None else (half * HALF, HALF)
        return rows.at[s, pl.ds(lo, n), lanes(col, COLS)]

    GZ = ((1, 0, 0), (1, 0, 1), (-1, 0, 1), (-1, 0, 0), (1, -1, 0), (-1, 1, 1))

    def gz_send(s, k):
        direction, shift, half = GZ[k]
        src = shard(s, shift, c, half)
        return rcopy(src, src, gz_ss.at[s, k], gz_rs.at[s, k], z_dev(direction + 4))

    def gz_wait(s, k):
        direction, shift, half = GZ[k]
        ref = shard(s, shift - direction, c, half)
        rcopy(ref, ref, gz_ss.at[s, k], gz_rs.at[s, k], z_dev(direction + 4)).wait_recv()

    GS = ((0, None), (-1, 0), (1, 1), (-1, 1), (1, 0), (2, 0), (2, 1))

    def gs_send(s, k):
        src = shard(s, GS[k][0], c, GS[k][1])
        return rcopy(src, src, gs_ss.at[s, k], gs_rs.at[s, k], sibling)

    def gs_wait(s, k):
        ref = shard(s, GS[k][0], 1 - c, GS[k][1])
        rcopy(ref, ref, gs_ss.at[s, k], gs_rs.at[s, k], sibling).wait_recv()

    def gather0(s):
        for k in (0, 2, 1, 3):
            gz_send(s, k).start()
        gs_send(s, 0).start()

    def gather1(s):
        gz_wait(s, 0)
        gz_send(s, 4).start()
        gs_send(s, 1).start()
        gz_wait(s, 2)
        gz_send(s, 5).start()
        gs_send(s, 2).start()

    def gather2(s):
        gz_wait(s, 1)
        gs_send(s, 3).start()
        gz_wait(s, 3)
        gs_send(s, 4).start()

    def gather3(s):
        gz_wait(s, 4)
        gs_send(s, 5).start()
        gz_wait(s, 5)
        gs_send(s, 6).start()

    def gather4(s):
        for k in range(7):
            gs_wait(s, k)

    def gather_drain(s):
        for k in range(6):
            gz_send(s, k).wait_send()
        for k in range(7):
            gs_send(s, k).wait_send()

    def hidden(s, weights):
        acc[...] = jnp.zeros_like(acc)

        def body(k, carry):
            x = rows[s, :, lanes(k * 1024, 1024)]
            acc[0] += jnp.dot(x, weights[pl.ds(k * 8, 8)].reshape(1024, 256), preferred_element_type=F32)
            acc[1] += jnp.dot(x, weights[pl.ds(56 + k * 8, 8)].reshape(1024, 256), preferred_element_type=F32)
            return carry

        lax.fori_loop(0, 7, body, 0)
        g = acc[0]
        return g / (1.0 + jnp.exp(-g)) * acc[1]

    def copy_tag():
        tag = tgi[...].astype(F32)
        return jnp.concatenate([tag, tag], axis=1)

    PARTS = ((0, 0, TILES), (1, 0, 4), (1, 4, 3))

    def own_cols(p):
        return pl.ds(PARTS[p][1] * 128, PARTS[p][2] * 128)

    def block_cols(p, zi, core):
        return lanes((((z + zi) % 4) * 2 + core) * COLS + PARTS[p][1] * 128, PARTS[p][2] * 128)

    def sib_copy(p, zi):
        s = PARTS[p][0]
        return rcopy(
            part.at[s, :, block_cols(p, zi, 1 - c)], sibr.at[s, zi, :, own_cols(p)],
            s_ss.at[p, zi], s_rs.at[p, zi], sibling,
        )

    def partials(p):
        s, first, count = PARTS[p]
        for zi in (2, 1, 3, 0):
            zz = (z + zi) % 4

            def body(q, carry, zz=zz):
                at = pl.ds(112 + 2 * (q * 4 + zz), 2)
                v = jnp.dot(hid[s], hw[at].reshape(256, 256), preferred_element_type=F32)
                if s == 1:
                    v += jnp.dot(hid[2], hot[at].reshape(256, 256), preferred_element_type=F32)
                v = v.astype(BF)
                for core in range(2):
                    part[s, :, lanes((zz * 2 + core) * COLS + q * 128, 128)] = v[:, core * 128 : (core + 1) * 128]
                return carry

            lax.fori_loop(first, first + count, body, 0)
            sib_copy(p, zi).start()

    def pair_sum(p, zi):
        s = PARTS[p][0]
        return part[s, :, block_cols(p, zi, c)].astype(F32) + sibr[s, zi, :, own_cols(p)].astype(F32)

    lo_half, hi_half = pl.ds(0, HALF), pl.ds(HALF, HALF)

    def z_copy(p, k):
        s, cols = PARTS[p][0], own_cols(p)
        src, dst, direction = (
            (zs.at[s, 0, lo_half, cols], za.at[s, :, cols], 1),
            (zs.at[s, 0, hi_half, cols], zb.at[s, :, cols], -1),
            (zs.at[s, 1, hi_half, cols], rp.at[s, hi_half, cols], 1),
            (zs.at[s, 1, lo_half, cols], rp.at[s, lo_half, cols], 1),
            (zs.at[s, 2, lo_half, cols], rm.at[s, lo_half, cols], -1),
            (zs.at[s, 2, hi_half, cols], rm.at[s, hi_half, cols], -1),
        )[k]
        return rcopy(src, dst, z_ss.at[p, k], z_rs.at[p, k], z_dev(direction + 4))

    def reduce1(p):
        s, cols = PARTS[p][0], own_cols(p)
        sib_copy(p, 2).wait_recv()
        zs[s, 0, :, cols] = pair_sum(p, 2).astype(BF)
        z_copy(p, 0).start()
        z_copy(p, 1).start()
        sib_copy(p, 1).wait_recv()
        zs[s, 1, :, cols] = pair_sum(p, 1).astype(BF)
        z_copy(p, 2).start()
        sib_copy(p, 3).wait_recv()
        zs[s, 2, :, cols] = pair_sum(p, 3).astype(BF)
        z_copy(p, 4).start()

    def reduce2(p):
        s, cols = PARTS[p][0], own_cols(p)
        z_copy(p, 0).wait_recv()
        zs[s, 1, lo_half, cols] = (zs[s, 1, lo_half, cols].astype(F32) + za[s, :, cols].astype(F32)).astype(BF)
        z_copy(p, 3).start()
        z_copy(p, 1).wait_recv()
        zs[s, 2, hi_half, cols] = (zs[s, 2, hi_half, cols].astype(F32) + zb[s, :, cols].astype(F32)).astype(BF)
        z_copy(p, 5).start()

    def reduce3(p):
        s, cols = PARTS[p][0], own_cols(p)
        sib_copy(p, 0).wait_recv()
        for k in (2, 4, 3, 5):
            z_copy(p, k).wait_recv()
        eo[s, :, cols] = (pair_sum(p, 0) + rp[s, :, cols].astype(F32) + rm[s, :, cols].astype(F32)).astype(BF)

    def reduce_drain(p):
        for zi in range(4):
            sib_copy(p, zi).wait_send()
        for k in range(6):
            z_copy(p, k).wait_send()

    def back_start(p):
        s, cols = PARTS[p][0], own_cols(p)

        def send(j, carry):
            peer = (e + j) % NE
            rcopy(
                eo.at[s, rows16(peer * CAP, CAP), cols], ret.at[rows16(s * SLOTS + e * CAP, CAP), cols],
                r_ss.at[p], r_rs.at[p], ep_dev(peer),
            ).start()
            return carry

        lax.fori_loop(1, NE, send, 0)
        ret[rows16(s * SLOTS + e * CAP, CAP), cols] = eo[s, rows16(e * CAP, CAP), cols]

    def back_wait(p):
        s, cols = PARTS[p][0], own_cols(p)
        n = (NE - 1) * CAP
        done = rcopy(
            eo.at[s, pl.ds(0, n), cols], ret.at[pl.ds(s * SLOTS, n), cols], r_ss.at[p], r_rs.at[p],
            ep_dev((e + 1) % NE),
        )
        done.wait_recv()
        done.wait_send()

    def final(p, j, at):
        peer = (w + j) % NW
        cols = own_cols(p)
        return rcopy(
            outb.at[rows16(peer * 16, 16), cols], fin.at[at, :, cols], f_ss.at[p - 1, j - 1], f_rs.at[p - 1, j - 1],
            wide_dev(peer),
        )

    def combine(p):
        cols = own_cols(p)
        outb[:, cols] = jnp.dot(wc[...], ret[:, cols], preferred_element_type=F32).astype(BF)
        for j in range(1, NW):
            final(p, j, w).start()
        fin[w, :, cols] = outb[rows16(w * 16, 16), cols]

    run(3)
    for j in range(1, NW):
        for copy in exchange(j, (w + j) % NW, (w + NW - j) % NW):
            copy.wait_recv()
    make_plan()
    a2a_start(0)
    run(1)
    a2a_start(1)
    run(4)
    a2a_wait(0)
    gather0(0)
    run(3)
    gather1(0)
    a2a_wait(1)
    run(3)
    gather2(0)
    gather0(1)
    run(3)
    gather3(0)
    run(1)
    gather4(0)
    hid[0] = hidden(0, hw).astype(BF)
    run(1)
    gather1(1)
    partials(0)
    run(2)
    gather2(1)
    reduce1(0)
    run(3)
    gather3(1)
    run(1)
    gather4(1)
    reduce2(0)
    run(1)
    hid[1] = (hidden(1, hw) * (1.0 - copy_tag())).astype(BF)
    run(3)
    reduce3(0)
    run_to(4 * LAG + FIRST)
    hid[2] = (hidden(1, hot) * copy_tag()).astype(BF)
    run_to(4 * LAG + FIRST + 8)
    partials(1)
    run(1)
    reduce1(1)
    run(2)
    reduce2(1)
    run(T_STEPS)
    partials(2)
    back_start(0)
    reduce1(2)
    reduce3(1)
    back_start(1)
    reduce2(2)
    back_wait(0)
    back_wait(1)
    combine(1)
    reduce3(2)
    back_start(2)
    drain_slots()
    for j in range(1, NW):
        for copy in exchange(j, (w + j) % NW, w):
            copy.wait_send()
    for s in range(STEPS):
        gather_drain(s)
    for p in range(3):
        reduce_drain(p)
    back_wait(2)
    combine(2)
    for p in (1, 2):
        for j in range(1, NW):
            final(p, j, (w + NW - j) % NW).wait_recv()
    blocks = [fin[k].astype(F32) for k in range(NW)]
    for q in range(TILES):
        line = jnp.concatenate([block[:, q * 128 : (q + 1) * 128] for block in blocks], axis=1)
        for s in range(STEPS):
            out[s, :, q * 1024 : (q + 1) * 1024] = line[s * 8 : (s + 1) * 8].astype(BF)
    for p in (1, 2):
        for j in range(1, NW):
            final(p, j, w).wait_send()


def shards(
    requests, routes, gates, replica, placement, copy_plan, capacity, gate_proj, up_proj, down_proj
):
    vmem = pl.BlockSpec(memory_space=pltpu.VMEM)
    smem = pl.BlockSpec(memory_space=pltpu.SMEM)
    hbm = pl.BlockSpec(memory_space=pl.ANY)
    dma = pltpu.SemaphoreType.DMA
    return pl.pallas_call(
        layer_kernel,
        out_shape=jax.ShapeDtypeStruct(requests.shape, BF),
        in_specs=[vmem, vmem, vmem, vmem, smem, smem, smem, hbm, hbm, hbm],
        out_specs=vmem,
        scratch_shapes=[
            pltpu.VMEM((NW, 16, COLS), BF),
            pltpu.VMEM((16, 128), F32),
            pltpu.VMEM((NW, 16, COLS), BF),
            pltpu.VMEM((NW, 16, 128), F32),
            pltpu.VMEM((STEPS, SLOTS, COLS), BF),
            pltpu.VMEM((SLOTS, 128), BF),
            pltpu.VMEM((SLOTS, 128), BF),
            pltpu.VMEM((STEPS, SLOTS, D), BF),
            pltpu.VMEM((168, 128, 256), BF),
            pltpu.VMEM((168, 128, 256), BF),
            pltpu.VMEM((4, RING, 128, 256), BF),
            pltpu.VMEM((4, STAGE, 128, 256), BF),
            pltpu.VMEM((len(MASKS), 16, 256), BF),
            pltpu.VMEM((2, SLOTS, HID), F32),
            pltpu.VMEM((3, SLOTS, HID), BF),
            pltpu.VMEM((STEPS, SLOTS, D), BF),
            pltpu.VMEM((STEPS, 4, SLOTS, COLS), BF),
            pltpu.VMEM((STEPS, 3, SLOTS, COLS), BF),
            pltpu.VMEM((STEPS, HALF, COLS), BF),
            pltpu.VMEM((STEPS, HALF, COLS), BF),
            pltpu.VMEM((STEPS, SLOTS, COLS), BF),
            pltpu.VMEM((STEPS, SLOTS, COLS), BF),
            pltpu.VMEM((STEPS, SLOTS, COLS), BF),
            pltpu.VMEM((STEPS * SLOTS, COLS), BF),
            pltpu.VMEM((128, STEPS * SLOTS), BF),
            pltpu.VMEM((128, COLS), BF),
            pltpu.VMEM((NW, 16, COLS), BF),
            dma,
            dma((7,)), dma((7,)), dma((7,)), dma((7,)),
            dma((2,)), dma((2,)), dma, dma,
            dma((4, STAGE)), dma((4, RING)),
            dma((2, 6)), dma((2, 6)), dma((2, 7)), dma((2, 7)),
            dma((3, 4)), dma((3, 4)), dma((3, 6)), dma((3, 6)),
            dma((3,)), dma((3,)), dma((2, 7)), dma((2, 7)),
        ],
        compiler_params=pltpu.CompilerParams(
            collective_id=0, has_side_effects=True, vmem_limit_bytes=62 * 1024 * 1024
        ),
        name="expert_layer",
    )(
        requests, routes, gates, replica, placement, copy_plan, capacity,
        gate_proj.reshape(TILES, NW, 128, HID), up_proj.reshape(TILES, NW, 128, HID), down_proj.reshape(HID, D),
    )


def solution(mesh):
    rows = P(None, ("ep", "wide"), None)
    placed = (
        rows, rows, rows, P(("ep", "wide"), None), P(), P(), P(),
        P("ep", None, "wide"), P("ep", None, "wide"), P("ep", "wide", None),
    )
    return jax.shard_map(shards, mesh=mesh, in_specs=placed, out_specs=rows, check_vma=False)
```

time: 196 us -> 151 us (0.77)
  Pallas kernels: 181 us -> 145 us
  other arithmetic: 8.18 us -> 0 us
  between operations: 3.34 us -> 0.01 us
  local copies, waits for them, and re-layouts: 3.7 us -> 5.7 us
    pallas_call x1, Pallas kernels: 181 us -> 145 us  [shards(): pl.pallas_call(layer_kernel, out_shape=jax.ShapeDtypeStruct(requests.shap...]
    reduce_sum x3 -> x0, other arithmetic: 4.71 us -> none  [the longest x1 2.01 us: shards(): jnp.sum(jnp.where(slots == copy_plan[0], placement, 0), dtype=jnp.int32)]
    unnamed x1 -> x4, local copies, waits for them, and re-layouts: 1.64 us -> 5.7 us
    convert_element_type x5 -> x0, other arithmetic: 3.45 us -> none  [the longest x1 0.73 us: shards(): cand[None].astype(F32)]
where the time goes in v2:
time: 151 us
  Pallas kernels  145 us (96%)
  local copies, waits for them, and re-layouts  5.7 us (4%)
    pallas_call x1, Pallas kernels, shards(): pl.pallas_call(layer_kernel, out_shape=jax.ShapeDtypeStruct(requests.shap...  145 us
    unnamed x4, local copies, waits for them, and re-layouts  5.7 us

profile of v2, /device:TPU:1, one launch (start us, length us, event | category | flops | bytes accessed | tf_op | source)
XLA Modules:
  0.0 150.6 jit_solution(5766287461913738647)
XLA Ops:
  0.0 1.4 copy.12.gates
  1.4 1.3 copy.13.replica
  2.7 1.4 copy.11.routes
  4.1 144.9 %expert_layer.1 = bf16[2,8,7168]{2,1,0:T(8,128)(2,1)} custom-call(bf16[2,8,7168]{2,1,0:T(8,128)(2,1)} %req.1, s32[2,8,2]{2,1,0:T(8,128)} %copy.11.routes, bf16[2,8,2]{2,1,0:T(8,128)(2,1)} %copy.12.gates, s32[8,2]{1,0:T(8,128)} %copy.13.replica, s32[16]{0:T(128)} %placement.1, s32[4]{0:T(128)} %copy_plan.1, s32[2,16]{1,0:T(2,128)} %capacity.1, ...), custom_call_target="tpu_custom_call" | custom-call | tf_op jit(solution)/shard_map/expert_layer/pallas_call | solution.py:628
  149.0 1.6 %copy.15 = bf16[2,8,7168]{2,1,0:T(8,128)(2,1)} copy(bf16[2,8,7168]{2,1,0:T(8,128)(2,1)} %expert_layer.1) | data formatting | bytes 458752

commit v3 on v2

--- a/solution.py
+++ b/solution.py
@@ -133,7 +133,7 @@
     for s in range(STEPS):
         line = jnp.zeros((8, 128), F32)
         for i, ref in enumerate((routes[s], replica[...], gates[s])):
-            values = ref.astype(F32)
+            values = ref.astype(F32).T
             for k in range(2):
                 line = jnp.where(lane8 == 2 * i + k, jnp.broadcast_to(values[:, k : k + 1], (8, 128)), line)
         meta[s * 8 : (s + 1) * 8, :] = line
@@ -396,7 +396,7 @@
         for k in range(7):
             gs_send(s, k).wait_send()
 
-    def hidden(s, weights):
+    def hidden(s, weights, slots):
         acc[...] = jnp.zeros_like(acc)
 
         def body(k, carry):
@@ -405,7 +405,9 @@
             acc[1] += jnp.dot(x, weights[pl.ds(56 + k * 8, 8)].reshape(1024, 256), preferred_element_type=F32)
             return carry
 
-        lax.fori_loop(0, 7, body, 0)
+        for lo, hi in ((0, 2), (2, 4), (4, 6), (6, 7)):
+            lax.fori_loop(lo, hi, body, 0)
+            run(slots)
         g = acc[0]
         return g / (1.0 + jnp.exp(-g)) * acc[1]
 
@@ -413,7 +415,7 @@
         tag = tgi[...].astype(F32)
         return jnp.concatenate([tag, tag], axis=1)
 
-    PARTS = ((0, 0, TILES), (1, 0, 4), (1, 4, 3))
+    PARTS = ((0, 0, TILES), (1, 0, 3), (1, 3, 3), (1, 6, 1))
 
     def own_cols(p):
         return pl.ds(PARTS[p][1] * 128, PARTS[p][2] * 128)
@@ -428,12 +430,11 @@
             s_ss.at[p, zi], s_rs.at[p, zi], sibling,
         )
 
-    def partials(p):
+    def partials(p, slots):
         s, first, count = PARTS[p]
         for zi in (2, 1, 3, 0):
             zz = (z + zi) % 4
-
-            def body(q, carry, zz=zz):
+            for q in range(first, first + count):
                 at = pl.ds(112 + 2 * (q * 4 + zz), 2)
                 v = jnp.dot(hid[s], hw[at].reshape(256, 256), preferred_element_type=F32)
                 if s == 1:
@@ -441,10 +442,8 @@
                 v = v.astype(BF)
                 for core in range(2):
                     part[s, :, lanes((zz * 2 + core) * COLS + q * 128, 128)] = v[:, core * 128 : (core + 1) * 128]
-                return carry
-
-            lax.fori_loop(first, first + count, body, 0)
             sib_copy(p, zi).start()
+            run(slots)
 
     def pair_sum(p, zi):
         s = PARTS[p][0]
@@ -546,66 +545,70 @@
     a2a_start(0)
     run(1)
     a2a_start(1)
-    run(4)
+    run_to(9)
     a2a_wait(0)
     gather0(0)
-    run(3)
+    run_to(13)
     gather1(0)
     a2a_wait(1)
-    run(3)
+    run_to(17)
     gather2(0)
     gather0(1)
-    run(3)
+    run_to(20)
     gather3(0)
-    run(1)
+    run_to(21)
     gather4(0)
-    hid[0] = hidden(0, hw).astype(BF)
-    run(1)
+    hid[0] = hidden(0, hw, 1).astype(BF)
     gather1(1)
-    partials(0)
-    run(2)
+    partials(0, 1)
     gather2(1)
     reduce1(0)
-    run(3)
+    run_to(32)
     gather3(1)
-    run(1)
+    run_to(33)
     gather4(1)
+    hid[1] = (hidden(1, hw, 1) * (1.0 - copy_tag())).astype(BF)
     reduce2(0)
-    run(1)
-    hid[1] = (hidden(1, hw) * (1.0 - copy_tag())).astype(BF)
-    run(3)
+    run_to(4 * LAG + FIRST)
+    hid[2] = (hidden(1, hot, 1) * copy_tag()).astype(BF)
     reduce3(0)
-    run_to(4 * LAG + FIRST)
-    hid[2] = (hidden(1, hot) * copy_tag()).astype(BF)
-    run_to(4 * LAG + FIRST + 8)
-    partials(1)
-    run(1)
+    run_to(4 * LAG + FIRST + 6)
+    partials(1, 0)
+    run(2)
     reduce1(1)
     run(2)
     reduce2(1)
+    run_to(4 * LAG + FIRST + 12)
+    partials(2, 0)
     run(T_STEPS)
-    partials(2)
+    reduce1(2)
+    partials(3, 0)
+    reduce3(1)
     back_start(0)
-    reduce1(2)
-    reduce3(1)
     back_start(1)
     reduce2(2)
+    reduce1(3)
+    reduce2(3)
+    reduce3(2)
+    back_start(2)
     back_wait(0)
     back_wait(1)
     combine(1)
-    reduce3(2)
-    back_start(2)
+    reduce3(3)
+    back_start(3)
+    back_wait(2)
+    combine(2)
     drain_slots()
     for j in range(1, NW):
         for copy in exchange(j, (w + j) % NW, w):
             copy.wait_send()
     for s in range(STEPS):
         gather_drain(s)
-    for p in range(3):
+    for p in range(4):
         reduce_drain(p)
-    back_wait(2)
-    combine(2)
-    for p in (1, 2):
+    back_wait(3)
+    combine(3)
+    for p in (1, 2, 3):
         for j in range(1, NW):
             final(p, j, (w + NW - j) % NW).wait_recv()
     blocks = [fin[k].astype(F32) for k in range(NW)]
@@ -613,7 +616,7 @@
         line = jnp.concatenate([block[:, q * 128 : (q + 1) * 128] for block in blocks], axis=1)
         for s in range(STEPS):
             out[s, :, q * 1024 : (q + 1) * 1024] = line[s * 8 : (s + 1) * 8].astype(BF)
-    for p in (1, 2):
+    for p in (1, 2, 3):
         for j in range(1, NW):
             final(p, j, w).wait_send()
 
@@ -663,15 +666,15 @@
             dma((2,)), dma((2,)), dma, dma,
             dma((4, STAGE)), dma((4, RING)),
             dma((2, 6)), dma((2, 6)), dma((2, 7)), dma((2, 7)),
-            dma((3, 4)), dma((3, 4)), dma((3, 6)), dma((3, 6)),
-            dma((3,)), dma((3,)), dma((2, 7)), dma((2, 7)),
+            dma((4, 4)), dma((4, 4)), dma((4, 6)), dma((4, 6)),
+            dma((4,)), dma((4,)), dma((3, 7)), dma((3, 7)),
         ],
         compiler_params=pltpu.CompilerParams(
             collective_id=0, has_side_effects=True, vmem_limit_bytes=62 * 1024 * 1024
         ),
         name="expert_layer",
     )(
-        requests, routes, gates, replica, placement, copy_plan, capacity,
+        requests, jnp.swapaxes(routes, 1, 2), jnp.swapaxes(gates, 1, 2), replica.T, placement, copy_plan, capacity,
         gate_proj.reshape(TILES, NW, 128, HID), up_proj.reshape(TILES, NW, 128, HID), down_proj.reshape(HID, D),
     )
 

time: 151 us -> 128 us (0.85)
  Pallas kernels: 145 us -> 127 us
  local copies, waits for them, and re-layouts: 5.7 us -> 1.64 us
    pallas_call x1, Pallas kernels: 145 us -> 127 us  [shards(): pl.pallas_call(layer_kernel, out_shape=jax.ShapeDtypeStruct(requests.shap...]
    unnamed x4 -> x1, local copies, waits for them, and re-layouts: 5.7 us -> 1.64 us
where the time goes in v3:
time: 128 us
  Pallas kernels  127 us (99%)
  local copies, waits for them, and re-layouts  1.64 us (1%)
    pallas_call x1, Pallas kernels, shards(): pl.pallas_call(layer_kernel, out_shape=jax.ShapeDtypeStruct(requests.shap...  127 us

profile of v3, /device:TPU:1, one launch (start us, length us, event | category | flops | bytes accessed | tf_op | source)
XLA Modules:
  0.0 128.3 jit_solution(8340275992833890314)
XLA Ops:
  0.0 126.7 %expert_layer.1 = bf16[2,8,7168]{2,1,0:T(8,128)(2,1)} custom-call(bf16[2,8,7168]{2,1,0:T(8,128)(2,1)} %req.1, s32[2,2,8]{2,1,0:T(2,128)} %bitcast.9, bf16[2,2,8]{2,1,0:T(2,128)(2,1)} %bitcast.10, s32[2,8]{1,0:T(2,128)} %bitcast.11, s32[16]{0:T(128)} %placement.1, s32[4]{0:T(128)} %copy_plan.1, s32[2,16]{1,0:T(2,128)} %capacity.1, ...), custom_call_target="tpu_custom_call" | custom-call | tf_op jit(solution)/shard_map/expert_layer/pallas_call | solution.py:631
  126.7 1.6 %copy.12 = bf16[2,8,7168]{2,1,0:T(8,128)(2,1)} copy(bf16[2,8,7168]{2,1,0:T(8,128)(2,1)} %expert_layer.1) | data formatting | bytes 458752

commit v4 on v3

--- a/solution.py
+++ b/solution.py
@@ -27,13 +27,15 @@
     ((0, 0, 2), (0, 1, 1), (0, 1, 0), (0, 1, 2), (3, 1, 3), (1, 1, 3), (3, 1, 2), (3, 2, 2)),
     ((0, 0, 3), (0, 3, 3), (0, 3, 1), (0, 3, 0), (0, 2, 0), (3, 3, 2), (1, 3, 2), (1, 2, 3)),
 )
-LAG = 3
-CHUNKS = 42
-FIRST = 28
+LAG = 6
+CUT = 2
+CHUNK = 128 // CUT
+CHUNKS = 42 * CUT
+FIRST = 28 * CUT
 T_SLOTS = CHUNKS + 3 * LAG
 T_STEPS = CHUNKS + 4 * LAG
-STAGE = 4
-RING = 16
+STAGE = LAG + 1
+RING = 5 * LAG + 1
 
 
 def relay_tables():
@@ -174,11 +176,17 @@
             link_dev[link],
         )
 
-    def chunk_at(tree, n, later):
-        return 112 + ((n - FIRST) // 2 * 4 + tree) * 2 + n % 2 if later else tree * FIRST + n
+    def chunk_of(ref, tree, n, later):
+        block = n // CUT
+        if later:
+            block -= FIRST // CUT
+            block = 112 + (block // 2 * 4 + tree) * 2 + block % 2
+        else:
+            block += tree * (FIRST // CUT)
+        return ref.at[block, rows16(n % CUT * CHUNK, CHUNK)]
 
     def masked(block, mask):
-        return block.reshape(8, 16, 256) * mk[MASK_AT[mask]][None]
+        return block.reshape(CHUNK // 16, 16, 256) * mk[MASK_AT[mask]][None]
 
     def add(total, term):
         return term if total is None else total + term
@@ -197,10 +205,10 @@
                         continue
                     if k == link ^ 1:
                         if own:
-                            total = add(total, masked(hw[chunk_at(link, t, own_later)], ("relay", (link, k))))
+                            total = add(total, masked(chunk_of(hw, link, t, own_later)[...], ("relay", (link, k))))
                     elif recv:
                         total = add(total, masked(rb[k, (t - LAG) % RING], ("relay", (link, k))))
-                sb[link, t % STAGE] = total.reshape(128, 256)
+                sb[link, t % STAGE] = total.reshape(CHUNK, 256)
                 slot_copy(link, t).start()
         if deliver:
             n = t - 4 * LAG
@@ -209,7 +217,7 @@
                 for link, behind in sorted(ARRIVE[tree]):
                     block = rb[link, (n + behind) % RING]
                     total = add(total, masked(block, ("arrive", tree, (link, behind))))
-                hot[chunk_at(tree, n, deliver_later)] = total.reshape(128, 256)
+                chunk_of(hot, tree, n, deliver_later)[...] = total.reshape(CHUNK, 256)
 
     cursor = [0]
 
@@ -233,7 +241,7 @@
                 lax.fori_loop(lo, hi, body, 0)
 
     def run(count):
-        run_to(cursor[0] + count)
+        run_to(cursor[0] + count * CUT)
 
     def drain_slots():
         def drain_send(t, carry):
@@ -397,16 +405,13 @@
             gs_send(s, k).wait_send()
 
     def hidden(s, weights, slots):
-        acc[...] = jnp.zeros_like(acc)
-
-        def body(k, carry):
-            x = rows[s, :, lanes(k * 1024, 1024)]
-            acc[0] += jnp.dot(x, weights[pl.ds(k * 8, 8)].reshape(1024, 256), preferred_element_type=F32)
-            acc[1] += jnp.dot(x, weights[pl.ds(56 + k * 8, 8)].reshape(1024, 256), preferred_element_type=F32)
-            return carry
-
-        for lo, hi in ((0, 2), (2, 4), (4, 6), (6, 7)):
-            lax.fori_loop(lo, hi, body, 0)
+        for k in range(4):
+            x = rows[s, :, k * 1792 : (k + 1) * 1792]
+            for i in range(2):
+                v = jnp.dot(
+                    x, weights[56 * i + 14 * k : 56 * i + 14 * k + 14].reshape(1792, 256), preferred_element_type=F32
+                )
+                acc[i] = v if k == 0 else acc[i] + v
             run(slots)
         g = acc[0]
         return g / (1.0 + jnp.exp(-g)) * acc[1]
@@ -415,7 +420,7 @@
         tag = tgi[...].astype(F32)
         return jnp.concatenate([tag, tag], axis=1)
 
-    PARTS = ((0, 0, TILES), (1, 0, 3), (1, 3, 3), (1, 6, 1))
+    PARTS = ((0, 0, TILES), (1, 0, 2), (1, 2, 2), (1, 4, 2), (1, 6, 1))
 
     def own_cols(p):
         return pl.ds(PARTS[p][1] * 128, PARTS[p][2] * 128)
@@ -537,78 +542,86 @@
             final(p, j, w).start()
         fin[w, :, cols] = outb[rows16(w * 16, 16), cols]
 
-    run(3)
+    run(5)
     for j in range(1, NW):
         for copy in exchange(j, (w + j) % NW, (w + NW - j) % NW):
             copy.wait_recv()
     make_plan()
     a2a_start(0)
-    run(1)
-    a2a_start(1)
-    run_to(9)
+    run_to(8 * CUT)
     a2a_wait(0)
     gather0(0)
-    run_to(13)
+    a2a_start(1)
+    run_to(12 * CUT)
     gather1(0)
     a2a_wait(1)
-    run_to(17)
+    run_to(16 * CUT)
     gather2(0)
     gather0(1)
-    run_to(20)
+    run_to(19 * CUT)
     gather3(0)
-    run_to(21)
+    run_to(20 * CUT)
     gather4(0)
     hid[0] = hidden(0, hw, 1).astype(BF)
     gather1(1)
     partials(0, 1)
     gather2(1)
     reduce1(0)
-    run_to(32)
+    run_to(31 * CUT)
     gather3(1)
-    run_to(33)
+    run_to(32 * CUT)
     gather4(1)
     hid[1] = (hidden(1, hw, 1) * (1.0 - copy_tag())).astype(BF)
     reduce2(0)
     run_to(4 * LAG + FIRST)
     hid[2] = (hidden(1, hot, 1) * copy_tag()).astype(BF)
     reduce3(0)
-    run_to(4 * LAG + FIRST + 6)
+    run_to(4 * LAG + FIRST + 4 * CUT)
     partials(1, 0)
     run(2)
     reduce1(1)
-    run(2)
+    run_to(4 * LAG + FIRST + 8 * CUT)
+    partials(2, 0)
     reduce2(1)
-    run_to(4 * LAG + FIRST + 12)
-    partials(2, 0)
+    run(1)
+    reduce1(2)
+    run_to(4 * LAG + FIRST + 12 * CUT)
+    partials(3, 0)
+    reduce2(2)
+    run(1)
+    reduce1(3)
     run(T_STEPS)
-    reduce1(2)
-    partials(3, 0)
+    partials(4, 0)
     reduce3(1)
+    back_start(1)
+    reduce2(3)
+    reduce1(4)
     back_start(0)
-    back_start(1)
-    reduce2(2)
-    reduce1(3)
-    reduce2(3)
     reduce3(2)
     back_start(2)
+    reduce2(4)
+    reduce3(3)
+    back_start(3)
+    reduce3(4)
+    back_start(4)
     back_wait(0)
     back_wait(1)
     combine(1)
-    reduce3(3)
-    back_start(3)
     back_wait(2)
     combine(2)
+    back_wait(3)
+    combine(3)
     drain_slots()
     for j in range(1, NW):
         for copy in exchange(j, (w + j) % NW, w):
             copy.wait_send()
     for s in range(STEPS):
         gather_drain(s)
-    for p in range(4):
+    for p in range(5):
         reduce_drain(p)
-    back_wait(3)
-    combine(3)
-    for p in (1, 2, 3):
+    back_wait(4)
+    combine(4)
+    for p in (1, 2, 3, 4):
         for j in range(1, NW):
             final(p, j, (w + NW - j) % NW).wait_recv()
     blocks = [fin[k].astype(F32) for k in range(NW)]
@@ -616,7 +629,7 @@
         line = jnp.concatenate([block[:, q * 128 : (q + 1) * 128] for block in blocks], axis=1)
         for s in range(STEPS):
             out[s, :, q * 1024 : (q + 1) * 1024] = line[s * 8 : (s + 1) * 8].astype(BF)
-    for p in (1, 2, 3):
+    for p in (1, 2, 3, 4):
         for j in range(1, NW):
             final(p, j, w).wait_send()
 
@@ -644,8 +657,8 @@
             pltpu.VMEM((STEPS, SLOTS, D), BF),
             pltpu.VMEM((168, 128, 256), BF),
             pltpu.VMEM((168, 128, 256), BF),
-            pltpu.VMEM((4, RING, 128, 256), BF),
-            pltpu.VMEM((4, STAGE, 128, 256), BF),
+            pltpu.VMEM((4, RING, CHUNK, 256), BF),
+            pltpu.VMEM((4, STAGE, CHUNK, 256), BF),
             pltpu.VMEM((len(MASKS), 16, 256), BF),
             pltpu.VMEM((2, SLOTS, HID), F32),
             pltpu.VMEM((3, SLOTS, HID), BF),
@@ -666,8 +679,8 @@
             dma((2,)), dma((2,)), dma, dma,
             dma((4, STAGE)), dma((4, RING)),
             dma((2, 6)), dma((2, 6)), dma((2, 7)), dma((2, 7)),
-            dma((4, 4)), dma((4, 4)), dma((4, 6)), dma((4, 6)),
-            dma((4,)), dma((4,)), dma((3, 7)), dma((3, 7)),
+            dma((5, 4)), dma((5, 4)), dma((5, 6)), dma((5, 6)),
+            dma((5,)), dma((5,)), dma((4, 7)), dma((4, 7)),
         ],
         compiler_params=pltpu.CompilerParams(
             collective_id=0, has_side_effects=True, vmem_limit_bytes=62 * 1024 * 1024

time: 128 us -> 124 us (0.969)
  Pallas kernels: 127 us -> 123 us
    pallas_call x1, Pallas kernels: 127 us -> 123 us  [shards(): pl.pallas_call(layer_kernel, out_shape=jax.ShapeDtypeStruct(requests.shap...]
where the time goes in v4:
time: 124 us
  Pallas kernels  123 us (99%)
  local copies, waits for them, and re-layouts  1.64 us (1%)
    pallas_call x1, Pallas kernels, shards(): pl.pallas_call(layer_kernel, out_shape=jax.ShapeDtypeStruct(requests.shap...  123 us

profile of v4, /device:TPU:1, one launch (start us, length us, event | category | flops | bytes accessed | tf_op | source)
XLA Modules:
  0.0 124.3 jit_solution(8646099944110144195)
XLA Ops:
  0.0 122.7 %expert_layer.1 = bf16[2,8,7168]{2,1,0:T(8,128)(2,1)} custom-call(bf16[2,8,7168]{2,1,0:T(8,128)(2,1)} %req.1, s32[2,2,8]{2,1,0:T(2,128)} %bitcast.9, bf16[2,2,8]{2,1,0:T(2,128)(2,1)} %bitcast.10, s32[2,8]{1,0:T(2,128)} %bitcast.11, s32[16]{0:T(128)} %placement.1, s32[4]{0:T(128)} %copy_plan.1, s32[2,16]{1,0:T(2,128)} %capacity.1, ...), custom_call_target="tpu_custom_call" | custom-call | tf_op jit(solution)/shard_map/expert_layer/pallas_call | solution.py:644
  122.7 1.6 %copy.12 = bf16[2,8,7168]{2,1,0:T(8,128)(2,1)} copy(bf16[2,8,7168]{2,1,0:T(8,128)(2,1)} %expert_layer.1) | data formatting | bytes 458752

commit v5 on v4

--- a/solution.py
+++ b/solution.py
@@ -159,8 +159,8 @@
 
     def exchange(j, peer, at):
         return (
-            rcopy(xs.at[(w + j) % NW], xin.at[at], x_ss.at[j - 1], x_rs.at[j - 1], wide_dev(peer)),
-            rcopy(meta, xmeta.at[at], m_ss.at[j - 1], m_rs.at[j - 1], wide_dev(peer)),
+            rcopy(xs.at[(w + j) % NW], xin.at[at], x_ss, x_rs, wide_dev(peer)),
+            rcopy(meta, xmeta.at[at], m_ss, m_rs, wide_dev(peer)),
         )
 
     for j in range(1, NW):
@@ -454,13 +454,16 @@
         s = PARTS[p][0]
         return part[s, :, block_cols(p, zi, c)].astype(F32) + sibr[s, zi, :, own_cols(p)].astype(F32)
 
+    DIRECT = (4,)
+
     lo_half, hi_half = pl.ds(0, HALF), pl.ds(HALF, HALF)
 
     def z_copy(p, k):
         s, cols = PARTS[p][0], own_cols(p)
+        direct = p in DIRECT
         src, dst, direction = (
-            (zs.at[s, 0, lo_half, cols], za.at[s, :, cols], 1),
-            (zs.at[s, 0, hi_half, cols], zb.at[s, :, cols], -1),
+            (zs.at[s, 0, lo_half, cols], za.at[s, :, cols], 2 if direct else 1),
+            (zs.at[s, 0, hi_half, cols], zb.at[s, :, cols], 2 if direct else -1),
             (zs.at[s, 1, hi_half, cols], rp.at[s, hi_half, cols], 1),
             (zs.at[s, 1, lo_half, cols], rp.at[s, lo_half, cols], 1),
             (zs.at[s, 2, lo_half, cols], rm.at[s, lo_half, cols], -1),
@@ -477,9 +480,13 @@
         sib_copy(p, 1).wait_recv()
         zs[s, 1, :, cols] = pair_sum(p, 1).astype(BF)
         z_copy(p, 2).start()
+        if p in DIRECT:
+            z_copy(p, 3).start()
         sib_copy(p, 3).wait_recv()
         zs[s, 2, :, cols] = pair_sum(p, 3).astype(BF)
         z_copy(p, 4).start()
+        if p in DIRECT:
+            z_copy(p, 5).start()
 
     def reduce2(p):
         s, cols = PARTS[p][0], own_cols(p)
@@ -495,7 +502,12 @@
         sib_copy(p, 0).wait_recv()
         for k in (2, 4, 3, 5):
             z_copy(p, k).wait_recv()
-        eo[s, :, cols] = (pair_sum(p, 0) + rp[s, :, cols].astype(F32) + rm[s, :, cols].astype(F32)).astype(BF)
+        total = pair_sum(p, 0) + rp[s, :, cols].astype(F32) + rm[s, :, cols].astype(F32)
+        if p in DIRECT:
+            for k in (0, 1):
+                z_copy(p, k).wait_recv()
+            total += jnp.concatenate([za[s, :, cols].astype(F32), zb[s, :, cols].astype(F32)], axis=0)
+        eo[s, :, cols] = total.astype(BF)
 
     def reduce_drain(p):
         for zi in range(4):
@@ -531,9 +543,17 @@
         peer = (w + j) % NW
         cols = own_cols(p)
         return rcopy(
-            outb.at[rows16(peer * 16, 16), cols], fin.at[at, :, cols], f_ss.at[p - 1, j - 1], f_rs.at[p - 1, j - 1],
-            wide_dev(peer),
+            outb.at[rows16(peer * 16, 16), cols], fin.at[at, :, cols], f_ss.at[p - 1], f_rs.at[p - 1], wide_dev(peer)
         )
+
+    def wait_bytes(ref, sem):
+        pltpu.make_async_copy(ref, ref, sem).wait()
+
+    def final_wait(p):
+        wait_bytes(fin.at[pl.ds(0, NW - 1), :, own_cols(p)], f_rs.at[p - 1])
+
+    def final_drain(p):
+        wait_bytes(outb.at[pl.ds(0, (NW - 1) * 16), own_cols(p)], f_ss.at[p - 1])
 
     def combine(p):
         cols = own_cols(p)
@@ -543,9 +563,8 @@
         fin[w, :, cols] = outb[rows16(w * 16, 16), cols]
 
     run(5)
-    for j in range(1, NW):
-        for copy in exchange(j, (w + j) % NW, (w + NW - j) % NW):
-            copy.wait_recv()
+    wait_bytes(xin.at[pl.ds(0, NW - 1)], x_rs)
+    wait_bytes(xmeta.at[pl.ds(0, NW - 1)], m_rs)
     make_plan()
     a2a_start(0)
     run_to(8 * CUT)
@@ -585,6 +604,8 @@
     reduce2(1)
     run(1)
     reduce1(2)
+    run_to(T_SLOTS)
+    back_start(0)
     run_to(4 * LAG + FIRST + 12 * CUT)
     partials(3, 0)
     reduce2(2)
@@ -596,14 +617,17 @@
     back_start(1)
     reduce2(3)
     reduce1(4)
-    back_start(0)
     reduce3(2)
     back_start(2)
-    reduce2(4)
     reduce3(3)
     back_start(3)
     reduce3(4)
     back_start(4)
+    drain_slots()
+    wait_bytes(xs.at[pl.ds(0, NW - 1)], x_ss)
+    wait_bytes(xmeta.at[pl.ds(0, NW - 1)], m_ss)
+    for s in range(STEPS):
+        gather_drain(s)
     back_wait(0)
     back_wait(1)
     combine(1)
@@ -611,27 +635,23 @@
     combine(2)
     back_wait(3)
     combine(3)
-    drain_slots()
-    for j in range(1, NW):
-        for copy in exchange(j, (w + j) % NW, w):
-            copy.wait_send()
-    for s in range(STEPS):
-        gather_drain(s)
+    back_wait(4)
+    combine(4)
     for p in range(5):
         reduce_drain(p)
-    back_wait(4)
-    combine(4)
-    for p in (1, 2, 3, 4):
-        for j in range(1, NW):
-            final(p, j, (w + NW - j) % NW).wait_recv()
-    blocks = [fin[k].astype(F32) for k in range(NW)]
-    for q in range(TILES):
-        line = jnp.concatenate([block[:, q * 128 : (q + 1) * 128] for block in blocks], axis=1)
-        for s in range(STEPS):
-            out[s, :, q * 1024 : (q + 1) * 1024] = line[s * 8 : (s + 1) * 8].astype(BF)
-    for p in (1, 2, 3, 4):
-        for j in range(1, NW):
-            final(p, j, w).wait_send()
+
+    def store(first, count):
+        blocks = [fin[k, :, first * 128 : (first + count) * 128].astype(F32) for k in range(NW)]
+        for q in range(count):
+            line = jnp.concatenate([block[:, q * 128 : (q + 1) * 128] for block in blocks], axis=1)
+            for s in range(STEPS):
+                out[s, :, (first + q) * 1024 : (first + q + 1) * 1024] = line[s * 8 : (s + 1) * 8].astype(BF)
+
+    for p in range(1, 5):
+        final_wait(p)
+        store(PARTS[p][1], PARTS[p][2])
+    for p in range(1, 5):
+        final_drain(p)
 
 
 def shards(
@@ -675,12 +695,12 @@
             pltpu.VMEM((128, COLS), BF),
             pltpu.VMEM((NW, 16, COLS), BF),
             dma,
-            dma((7,)), dma((7,)), dma((7,)), dma((7,)),
+            dma, dma, dma, dma,
             dma((2,)), dma((2,)), dma, dma,
             dma((4, STAGE)), dma((4, RING)),
             dma((2, 6)), dma((2, 6)), dma((2, 7)), dma((2, 7)),
             dma((5, 4)), dma((5, 4)), dma((5, 6)), dma((5, 6)),
-            dma((5,)), dma((5,)), dma((4, 7)), dma((4, 7)),
+            dma((5,)), dma((5,)), dma((4,)), dma((4,)),
         ],
         compiler_params=pltpu.CompilerParams(
             collective_id=0, has_side_effects=True, vmem_limit_bytes=62 * 1024 * 1024

time: 124 us -> 121 us (0.976)
  Pallas kernels: 123 us -> 119 us
    pallas_call x1, Pallas kernels: 123 us -> 119 us  [shards(): pl.pallas_call(layer_kernel, out_shape=jax.ShapeDtypeStruct(requests.shap...]
where the time goes in v5:
time: 121 us; the launch traced here: 120 us
  Pallas kernels  119 us (98%)
  local copies, waits for them, and re-layouts  1.64 us (1%)
    pallas_call x1, Pallas kernels, shards(): pl.pallas_call(layer_kernel, out_shape=jax.ShapeDtypeStruct(requests.shap...  119 us

profile of v5, /device:TPU:1, one launch (start us, length us, event | category | flops | bytes accessed | tf_op | source)
XLA Modules:
  0.0 120.4 jit_solution(17997221584428638096)
XLA Ops:
  0.0 118.8 %expert_layer.1 = bf16[2,8,7168]{2,1,0:T(8,128)(2,1)} custom-call(bf16[2,8,7168]{2,1,0:T(8,128)(2,1)} %req.1, s32[2,2,8]{2,1,0:T(2,128)} %bitcast.9, bf16[2,2,8]{2,1,0:T(2,128)(2,1)} %bitcast.10, s32[2,8]{1,0:T(2,128)} %bitcast.11, s32[16]{0:T(128)} %placement.1, s32[4]{0:T(128)} %copy_plan.1, s32[2,16]{1,0:T(2,128)} %capacity.1, ...), custom_call_target="tpu_custom_call" | custom-call | tf_op jit(solution)/shard_map/expert_layer/pallas_call | solution.py:664
  118.8 1.6 %copy.12 = bf16[2,8,7168]{2,1,0:T(8,128)(2,1)} copy(bf16[2,8,7168]{2,1,0:T(8,128)(2,1)} %expert_layer.1) | data formatting | bytes 458752

commit v6 on v5

--- a/solution.py
+++ b/solution.py
@@ -562,16 +562,16 @@
             final(p, j, w).start()
         fin[w, :, cols] = outb[rows16(w * 16, 16), cols]
 
-    run(5)
+    run(6)
     wait_bytes(xin.at[pl.ds(0, NW - 1)], x_rs)
     wait_bytes(xmeta.at[pl.ds(0, NW - 1)], m_rs)
     make_plan()
     a2a_start(0)
-    run_to(8 * CUT)
+    run_to(9 * CUT)
     a2a_wait(0)
     gather0(0)
     a2a_start(1)
-    run_to(12 * CUT)
+    run_to(13 * CUT)
     gather1(0)
     a2a_wait(1)
     run_to(16 * CUT)
@@ -623,11 +623,6 @@
     back_start(3)
     reduce3(4)
     back_start(4)
-    drain_slots()
-    wait_bytes(xs.at[pl.ds(0, NW - 1)], x_ss)
-    wait_bytes(xmeta.at[pl.ds(0, NW - 1)], m_ss)
-    for s in range(STEPS):
-        gather_drain(s)
     back_wait(0)
     back_wait(1)
     combine(1)
@@ -637,6 +632,11 @@
     combine(3)
     back_wait(4)
     combine(4)
+    drain_slots()
+    wait_bytes(xs.at[pl.ds(0, NW - 1)], x_ss)
+    wait_bytes(xmeta.at[pl.ds(0, NW - 1)], m_ss)
+    for s in range(STEPS):
+        gather_drain(s)
     for p in range(5):
         reduce_drain(p)
 

time: 121 us -> 121 us (level)
  no operation moved by 1% of the time
where the time goes in v6:
time: 121 us; the launch traced here: 120 us
  Pallas kernels  119 us (98%)
  local copies, waits for them, and re-layouts  1.64 us (1%)
    pallas_call x1, Pallas kernels, shards(): pl.pallas_call(layer_kernel, out_shape=jax.ShapeDtypeStruct(requests.shap...  119 us

profile of v6, /device:TPU:1, one launch (start us, length us, event | category | flops | bytes accessed | tf_op | source)
XLA Modules:
  0.0 120.4 jit_solution(6827334105183599514)
XLA Ops:
  0.0 118.8 %expert_layer.1 = bf16[2,8,7168]{2,1,0:T(8,128)(2,1)} custom-call(bf16[2,8,7168]{2,1,0:T(8,128)(2,1)} %req.1, s32[2,2,8]{2,1,0:T(2,128)} %bitcast.9, bf16[2,2,8]{2,1,0:T(2,128)(2,1)} %bitcast.10, s32[2,8]{1,0:T(2,128)} %bitcast.11, s32[16]{0:T(128)} %placement.1, s32[4]{0:T(128)} %copy_plan.1, s32[2,16]{1,0:T(2,128)} %capacity.1, ...), custom_call_target="tpu_custom_call" | custom-call | tf_op jit(solution)/shard_map/expert_layer/pallas_call | solution.py:664
  118.8 1.6 %copy.12 = bf16[2,8,7168]{2,1,0:T(8,128)(2,1)} copy(bf16[2,8,7168]{2,1,0:T(8,128)(2,1)} %expert_layer.1) | data formatting | bytes 458752
